TPU v7x, 256 devices: a whole 4x4x8 slice. The times are simulated.
256 devices in a mesh: dom: 32 (over x, z), col: 8 (over y, core).
Axes of the slice: x: 4, y: 4, z: 8, core: 2. Of those that a mesh axis runs over, the one named last changes fastest.
Arguments:
- band_tiles: float32 [6144, 128, 128], P(('dom', 'col')), may hold values from -0.1875 to 0.1875
- band_rows: int32 [6144], P(('dom', 'col')), may hold values from 0 to 31
- band_cols: int32 [6144], P(('dom', 'col')), may hold values from 0 to 47
- hub_tiles: float32 [2048, 128, 128], P(('dom', 'col')), may hold values from -0.1875 to 0.1875
- hub_rows: int32 [2048], P(('dom', 'col')), may hold values from 0 to 31
- hub_slots: int32 [2048], P(('dom', 'col')), may hold values from 0 to 31
- hub_blocks: int32 [32], replicated, may hold values from 0 to 1023, as said below
- start_vectors: float32 [131072, 64], P(('dom', 'col'))
- prior_directions: float32 [131072, 64], P(('dom', 'col'))
- rotation: float32 [2, 192, 64], replicated, as said below
Outputs:
- final_vectors: float32 [131072, 64], P(('dom', 'col'))
- final_directions: float32 [131072, 64], P(('dom', 'col'))
- ritz_block: float32 [64, 64], replicated
Inputs may be any that keep to these rules, and one draw needn't show every extreme that they name: hub_blocks[p] lies in panel p, between p * 32 and p * 32 + 31. Each rotation[i] has full column rank.
All inputs are finite; a program needn't handle non-finite values.
Results may differ from a plain program's by a relative error of at most 0.0034.
Values sent between devices are 32-bit elements; how exact they have to be, the bound alone decides.
A program may use at most 64 MiB of HBM per device.

v0:
```python
import jax
import jax.numpy as jnp
from jax import lax
from jax.sharding import PartitionSpec as P

TB = 128
K = 64
PB = 32
ITERS = 2
HW = 8


def extended_2(block, sides, width):
    for axis, dim in sides:
        count = lax.axis_size(axis)
        forward = [(i, i + 1) for i in range(count - 1)]
        forward.append((count - 1, 0))
        backward = [(target, source) for source, target in forward]
        low = lax.ppermute(
            lax.slice_in_dim(block, block.shape[dim] - width, None, axis=dim), axis, forward
        )
        high = lax.ppermute(lax.slice_in_dim(block, 0, width, axis=dim), axis, backward)
        block = jnp.concatenate([low, block, high], axis=dim)
    return block


def rotate(basis, gram_matrix, coeffs):
    highest = lax.Precision.HIGHEST
    reduced = jnp.dot(jnp.dot(coeffs.T, gram_matrix, precision=highest), coeffs, precision=highest)
    factor = jnp.linalg.cholesky(reduced)
    identity = jnp.eye(K, dtype=reduced.dtype)
    inverse = lax.linalg.triangular_solve(factor, identity, left_side=True, lower=True)
    new_vectors = jnp.dot(jnp.dot(basis, coeffs, precision=highest), inverse.T, precision=highest)
    new_directions = jnp.dot(
        jnp.dot(basis[:, K:], coeffs[K:], precision=highest), inverse.T, precision=highest
    )
    return (new_vectors, new_directions)


def per_device(
    band_tiles,
    band_rows,
    band_cols,
    hub_tiles,
    hub_rows,
    hub_slots,
    hub_blocks,
    start_vectors,
    prior_directions,
    rotation,
):
    highest = lax.Precision.HIGHEST
    panel_index = jnp.arange(PB, dtype=jnp.int32)
    band_onehot = (band_rows[None, :] == panel_index[:, None]).astype(jnp.float32)
    hub_onehot = (hub_rows[None, :] == panel_index[:, None]).astype(jnp.float32)
    shard_blocks = PB // lax.axis_size("col")
    vectors, directions = (start_vectors, prior_directions)
    ritz_block = jnp.zeros((K, K), jnp.float32)
    for step in range(ITERS):
        panel = lax.all_gather(vectors, "col", axis=0, tiled=True)
        extended = extended_2(panel, (("dom", 0),), HW * TB)
        blocks = extended.reshape(PB + 2 * HW, TB, K)
        picked = blocks[band_cols]
        products = jnp.einsum("tij,tjc->tic", band_tiles, picked, precision=highest)
        partial_value = jnp.einsum("rt,tic->ric", band_onehot, products, precision=highest)
        own_blocks = vectors.reshape(shard_blocks, TB, K)
        first_block = lax.axis_index("dom") * PB + lax.axis_index("col") * shard_blocks
        owned = first_block + jnp.arange(shard_blocks, dtype=jnp.int32)
        selector = (hub_blocks[:, None] == owned[None, :]).astype(jnp.float32)
        placed = jnp.einsum("hb,bic->hic", selector, own_blocks, precision=highest)
        hub_vectors = lax.psum(placed, ("dom", "col"))
        hub_products = jnp.einsum(
            "tij,tjc->tic", hub_tiles, hub_vectors[hub_slots], precision=highest
        )
        partial_value = partial_value + jnp.einsum(
            "rt,tic->ric", hub_onehot, hub_products, precision=highest
        )
        image = vectors - lax.psum_scatter(
            partial_value.reshape(PB * TB, K), "col", scatter_dimension=0, tiled=True
        )
        ritz_block = lax.psum(jnp.dot(vectors.T, image, precision=highest), ("dom", "col"))
        residual = image - jnp.dot(vectors, ritz_block, precision=highest)
        basis = jnp.concatenate([vectors, residual, directions], axis=1)
        gram_matrix = lax.psum(jnp.dot(basis.T, basis, precision=highest), ("dom", "col"))
        vectors, directions = rotate(basis, gram_matrix, rotation[step])
    return (vectors, directions, ritz_block)


def solution(mesh):
    return jax.shard_map(
        per_device,
        mesh=mesh,
        in_specs=(
            P(("dom", "col"), None, None),
            P(("dom", "col")),
            P(("dom", "col")),
            P(("dom", "col"), None, None),
            P(("dom", "col")),
            P(("dom", "col")),
            P(),
            P(("dom", "col"), None),
            P(("dom", "col"), None),
            P(),
        ),
        out_specs=(P(("dom", "col"), None), P(("dom", "col"), None), P()),
        check_vma=False,
    )
```

profile of v0, /device:TPU:1, one launch (start us, length us, event | category | flops | bytes accessed | tf_op | source)
XLA Modules:
  0.0 1319.3 jit_solution(8312204750492678957)
XLA Ops:
  9.8 2.3 fusion.61
  12.2 28.7 %all-gather.3.cloned.1.call-done = f32[4096,64]{0,1:T(8,128)} async-done(((f32[512,64]{0,1:T(8,128)}), f32[4096,64]{0,1:T(8,128)}) %all-gather.3.cloned.1.call-update) | async-done | bytes 1048592 | tf_op jit(solution)/shard_map/all_gather | solution.py:60
  42.8 5.2 collective-permute-start.1
  48.0 225.4 %all-reduce.5.cloned.1.call-done = f32[32,128,64]{1,0,2:T(8,128)} async-done(((f32[32,128,64]{1,0,2:T(8,128)}), f32[32,128,64]{1,0,2:T(8,128)}) %all-reduce.5.cloned.1.call-update) | async-done | bytes 1048592 | tf_op jit(solution)/shard_map/psum | solution.py:71
  273.4 2.8 copy.30
  280.0 2.4 copy_bitcast_fusion.1
  282.4 2.0 gather_fusion
  284.4 3.1 convolution_bitcast_fusion.1
  291.1 32.3 %reduce-scatter.3.cloned.1.call-done = f32[512,64]{0,1:T(8,128)} async-done(((f32[4096,64]{0,1:T(8,128)}), f32[512,64]{0,1:T(8,128)}) %reduce-scatter.3.cloned.1.call-update) | async-done | bytes 131088 | tf_op jit(solution)/shard_map/reduce_scatter | solution.py:78
  324.6 78.5 %psum.43 = f32[64,64]{0,1:T(8,128)S(1)} all-reduce(f32[64,64]{0,1:T(8,128)S(1)} %convolution_bitcast_fusion.5), channel_id=1, replica_groups=mesh['dom'=32,'col'=8] {'dom','col'}, use_global_device_ids=true, to_apply=%region_2.0 | all-reduce | flops 4096 | bytes 32768 | tf_op jit(solution)/shard_map/psum | solution.py:81
  405.2 241.7 %all-reduce.7.cloned.1.call-done = f32[192,192]{1,0:T(8,128)} async-done(((f32[192,192]{1,0:T(8,128)}), f32[192,192]{1,0:T(8,128)}) %all-reduce.7.cloned.1.call-update) | async-done | bytes 147472 | tf_op jit(solution)/shard_map/psum | solution.py:84
  648.5 5.8 cholesky.44
  655.6 4.9 custom-call.6
  664.5 22.6 %all-gather.5.cloned.1.call-done = f32[4096,64]{0,1:T(8,128)} async-done(((f32[512,64]{0,1:T(8,128)}), f32[4096,64]{0,1:T(8,128)}) %all-gather.5.cloned.1.call-update) | async-done | bytes 1048592 | tf_op jit(solution)/shard_map/all_gather | solution.py:60
  689.0 5.1 collective-permute-start.3
  694.1 228.2 %all-reduce.9.cloned.1.call-done = f32[32,128,64]{1,0,2:T(8,128)} async-done(((f32[32,128,64]{1,0,2:T(8,128)}), f32[32,128,64]{1,0,2:T(8,128)}) %all-reduce.9.cloned.1.call-update) | async-done | bytes 1048592 | tf_op jit(solution)/shard_map/psum | solution.py:71
  922.3 2.8 copy.35
  928.8 2.4 copy_bitcast_fusion
  933.3 3.1 convolution_bitcast_fusion
  940.7 31.6 %reduce-scatter.5.cloned.1.call-done = f32[512,64]{0,1:T(8,128)} async-done(((f32[4096,64]{0,1:T(8,128)}), f32[512,64]{0,1:T(8,128)}) %reduce-scatter.5.cloned.1.call-update) | async-done | bytes 131088 | tf_op jit(solution)/shard_map/reduce_scatter | solution.py:78
  973.5 78.8 %psum.46 = f32[64,64]{1,0:T(8,128)S(1)} all-reduce(f32[64,64]{1,0:T(8,128)S(1)} %fusion.78), channel_id=1, replica_groups=mesh['dom'=32,'col'=8] {'dom','col'}, use_global_device_ids=true, to_apply=%region_8.11 | all-reduce | flops 4096 | bytes 32768 | tf_op jit(solution)/shard_map/psum | solution.py:81
  1054.5 241.7 %all-reduce.11.cloned.1.call-done = f32[192,192]{1,0:T(8,128)} async-done(((f32[192,192]{1,0:T(8,128)}), f32[192,192]{1,0:T(8,128)}) %all-reduce.11.cloned.1.call-update) | async-done | bytes 147472 | tf_op jit(solution)/shard_map/psum | solution.py:84
  1297.7 5.8 cholesky.55
  1304.9 4.9 custom-call.7
  (119 shorter events, 40.9 us)
Async XLA Ops:
  8.0 276.4 %copy-start = (f32[24,128,128]{2,1,0:T(8,128)S(1)}, f32[24,128,128]{2,1,0:T(8,128)}, u32[]{:S(2)}) copy-start(f32[24,128,128]{2,1,0:T(8,128)} %param.13) | copy-start | bytes 4718596
  8.0 4.2 copy-start.20
  8.0 4.2 copy-start.21
  8.0 32.9 %all-gather.3.cloned.1.call-start = ((), (), s32[]{:S(2)}) async-start(), calls=%async_computation.2 | async-start | bytes 1179648 | tf_op jit(solution)/shard_map/all_gather | solution.py:60
  8.8 264.7 %all-reduce.5.cloned.1.call-start = ((), (), s32[]{:S(2)}) async-start(), calls=%async_computation.3 | async-start | bytes 2097152 | tf_op jit(solution)/shard_map/psum | solution.py:71
  12.1 311.3 %reduce-scatter.3.cloned.1.call-start = ((), (), s32[]{:S(2)}) async-start(), calls=%async_computation.4 | async-start | bytes 1179648 | tf_op jit(solution)/shard_map/reduce_scatter | solution.py:78
  42.8 237.1 %collective-permute-start.1 = (f32[1024,64]{0,1:T(8,128)}, f32[1024,64]{0,1:T(8,128)}, u32[]{:S(2)}, u32[]{:S(2)}) collective-permute-start(f32[1024,64]{0,1:T(8,128)} %get-tuple-element.8), channel_id=1, source_target_pairs={{8,0},{16,8},{24,16},{32,24},{40,32},{48,40},{56,48},{64,56},{72,6... | collective-permute-start | bytes 786440 | tf_op jit(solution)/shard_map/ppermute | solution.py:22
  48.0 232.0 %collective-permute-start = (f32[1024,64]{0,1:T(8,128)}, f32[1024,64]{0,1:T(8,128)}, u32[]{:S(2)}, u32[]{:S(2)}) collective-permute-start(f32[1024,64]{0,1:T(8,128)} %get-tuple-element.7), channel_id=1, source_target_pairs={{0,8},{8,16},{16,24},{24,32},{32,40},{40,48},{48,56},{56,64},{64,7... | collective-permute-start | bytes 786440 | tf_op jit(solution)/shard_map/ppermute | solution.py:19
  48.0 230.1 %copy-start.5 = (f32[8,128,128]{2,1,0:T(8,128)S(1)}, f32[8,128,128]{2,1,0:T(8,128)}, u32[]{:S(2)}) copy-start(f32[8,128,128]{2,1,0:T(8,128)} %param.16) | copy-start | bytes 1572868
  289.5 33.9 %copy-start.2 = (f32[512,64]{0,1:T(8,128)S(1)}, f32[512,64]{0,1:T(8,128)}, u32[]{:S(2)}) copy-start(f32[512,64]{0,1:T(8,128)} %param.20) | copy-start | bytes 393220
  291.1 112.3 %copy-start.11 = (f32[512,64]{0,1:T(8,128)S(1)}, f32[512,64]{0,1:T(8,128)}, u32[]{:S(2)}) copy-start(f32[512,64]{0,1:T(8,128)} %param.21) | copy-start | bytes 393220
  291.1 113.8 %copy-start.6 = (f32[2,192,64]{1,2,0:T(8,128)S(1)}, f32[2,192,64]{1,2,0:T(8,128)}, u32[]{:S(2)}) copy-start(f32[2,192,64]{1,2,0:T(8,128)} %param.22) | copy-start | bytes 294916
  291.1 355.9 %all-reduce.7.cloned.1.call-start = ((), (), s32[]{:S(2)}) async-start(), calls=%async_computation.5 | async-start | bytes 393216 | tf_op jit(solution)/shard_map/psum | solution.py:84
  403.1 259.7 %copy-start.16 = (s32[32]{0:T(128)S(1)}, s32[32]{0:T(128)}, u32[]{:S(2)}) copy-start(s32[32]{0:T(128)} %param.19) | copy-start | bytes 388
  403.4 261.1 %copy-start.7 = (f32[512,64]{0,1:T(8,128)}, f32[512,64]{0,1:T(8,128)S(1)}, u32[]{:S(2)}) copy-start(f32[512,64]{0,1:T(8,128)S(1)} %fusion) | copy-start | bytes 393220
  404.6 282.5 %all-gather.5.cloned.1.call-start = ((), (), s32[]{:S(2)}) async-start(), calls=%async_computation.6 | async-start | bytes 1179648 | tf_op jit(solution)/shard_map/all_gather | solution.py:60
  660.8 28.2 %copy-start.13 = (f32[64,64]{1,0:T(8,128)}, f32[64,64]{1,0:T(8,128)S(1)}, u32[]{:S(2)}) copy-start(f32[64,64]{1,0:T(8,128)S(1)} %fusion.37) | copy-start | bytes 49156
  661.8 260.6 %all-reduce.9.cloned.1.call-start = ((), (), s32[]{:S(2)}) async-start(), calls=%async_computation.7 | async-start | bytes 2097152 | tf_op jit(solution)/shard_map/psum | solution.py:71
  664.5 307.8 %reduce-scatter.5.cloned.1.call-start = ((), (), s32[]{:S(2)}) async-start(), calls=%async_computation.8 | async-start | bytes 1179648 | tf_op jit(solution)/shard_map/reduce_scatter | solution.py:78
  689.0 239.8 %collective-permute-start.3 = (f32[1024,64]{0,1:T(8,128)}, f32[1024,64]{0,1:T(8,128)}, u32[]{:S(2)}, u32[]{:S(2)}) collective-permute-start(f32[1024,64]{0,1:T(8,128)} %get-tuple-element.6), channel_id=1, source_target_pairs={{8,0},{16,8},{24,16},{32,24},{40,32},{48,40},{56,48},{64,56},{72,6... | collective-permute-start | bytes 786440 | tf_op jit(solution)/shard_map/ppermute | solution.py:22
  694.1 234.7 %collective-permute-start.2 = (f32[1024,64]{0,1:T(8,128)}, f32[1024,64]{0,1:T(8,128)}, u32[]{:S(2)}, u32[]{:S(2)}) collective-permute-start(f32[1024,64]{0,1:T(8,128)} %get-tuple-element.5), channel_id=1, source_target_pairs={{0,8},{8,16},{16,24},{24,32},{32,40},{40,48},{48,56},{56,64},{64,7... | collective-permute-start | bytes 786440 | tf_op jit(solution)/shard_map/ppermute | solution.py:19
  938.4 34.0 %copy-start.1 = (f32[512,64]{0,1:T(8,128)S(1)}, f32[512,64]{0,1:T(8,128)}, u32[]{:S(2)}) copy-start(f32[512,64]{0,1:T(8,128)} %fusion.77) | copy-start | bytes 393220
  940.0 356.3 %all-reduce.11.cloned.1.call-start = ((), (), s32[]{:S(2)}) async-start(), calls=%async_computation.9 | async-start | bytes 393216 | tf_op jit(solution)/shard_map/psum | solution.py:84
  1052.3 258.8 %copy-start.15 = (f32[64,64]{1,0:T(8,128)}, f32[64,64]{1,0:T(8,128)S(1)}, u32[]{:S(2)}) copy-start(f32[64,64]{1,0:T(8,128)S(1)} %psum.46) | copy-start | bytes 49156
  (10 other events, 22.7 us)
Sparse Core Ops, SparseCore 0:
  10.7 30.1 all-gather.2
  291.2 32.1 reduce-scatter.2
  661.9 25.2 all-gather.4
  940.1 32.1 reduce-scatter.4
Sparse Core Ops, SparseCore 1:
  14.7 258.7 all-reduce.4
  404.7 242.2 all-reduce.6
  668.6 253.7 all-reduce.8
  1054.3 241.9 all-reduce.10
where the time goes:
time: 1320 us
  waiting for transfers between devices  1050 us (80%)
  blocking collectives  157 us (12%)
  other arithmetic  30.9 us (2%)
  matrix products  28.8 us (2%)
  local copies, waits for them, and re-layouts  22.5 us (2%)
  between operations  16 us (1%)
    psum x2, waiting for transfers between devices, per_device(): lax.psum(jnp.dot(basis.T, basis, precision=highest), ('dom', 'col'))  483 us
    psum x2, waiting for transfers between devices, per_device(): hub_vectors = lax.psum(placed, ('dom', 'col'))  454 us
    psum x2, blocking collectives, per_device(): lax.psum(jnp.dot(vectors.T, image, precision=highest), ('dom', 'col'))  157 us
    reduce_scatter x2, waiting for transfers between devices, per_device(): lax.psum_scatter(partial_value.reshape(PB * TB, K), 'col', scatter_dimens...  63.9 us
    all_gather x2, waiting for transfers between devices, per_device(): panel = lax.all_gather(vectors, 'col', axis=0, tiled=True)  51.3 us
  transfers between devices with their start and end apart: 12, of which 8 were waited for; matrix products, arithmetic and copies ran while one was open for 2% of the time, Pallas kernels for 0%

commit v1 on v0

v1 whole, which is shorter than its diff:
```python
import jax
import jax.numpy as jnp
from jax import lax
from jax.experimental import pallas as pl
from jax.experimental.pallas import tpu as pltpu
from jax.sharding import PartitionSpec as P

TB = 128
K = 64
PB = 32
ITERS = 2
HW = 8
NZ = 8
NX = 4
NY = 4
N_DOM = 32
N_COL = 8
TPD = 24
HTD = 8
NT = TPD + HTD
OWN = 4
EXT = PB + 2 * HW
HUBS = 32
MESH = pl.DeviceIdType.MESH
F32 = jnp.float32
BF16 = jnp.bfloat16
HI = lax.Precision.HIGHEST


def wrap(value, count):
    return lax.rem(value + count, count)


def nn(a, b):
    return jnp.dot(a, b, precision=HI, preferred_element_type=F32)


def nt(a, b):
    return lax.dot_general(a, b, (((1,), (1,)), ((), ())), precision=HI, preferred_element_type=F32)


def split(value):
    high = value.astype(BF16)
    return high, (value - high.astype(F32)).astype(BF16)


def eliminate(matrix):
    rows = lax.broadcasted_iota(jnp.int32, (8, 2 * K), 0)
    lanes = lax.broadcasted_iota(jnp.int32, (8, 2 * K), 1)
    wide = jnp.concatenate([matrix, jnp.zeros((K, K), F32)], axis=1)
    blocks = [
        jnp.where(lanes - K == rows + 8 * b, 1.0, wide[8 * b : 8 * b + 8]) for b in range(K // 8)
    ]
    for k in range(K):
        home = k // 8
        row = jnp.broadcast_to(blocks[home][k % 8 : k % 8 + 1, :], (8, 2 * K))
        pivot = jnp.broadcast_to(row[:, k : k + 1], (8, 2 * K))
        scaled = row / pivot
        for b in range(home, K // 8):
            column = jnp.broadcast_to(blocks[b][:, k : k + 1], (8, 2 * K))
            if b == home:
                column = jnp.where(rows > k % 8, column, 0.0)
                own = row * lax.rsqrt(pivot)
                blocks[b] = jnp.where(rows == k % 8, own, blocks[b] - column * scaled)
            else:
                blocks[b] = blocks[b] - column * scaled
    return jnp.concatenate(blocks, axis=0)[:, K:]


def kernel(
    idx, flt, vec_in, dir_in, rot, band_hbm, hub_hbm,
    vec_out, dir_out, ritz_out,
    tiles, weights, state, image, own, ext, cand, hca, hubx, prods, ssend, srecv, rsum, rrecv,
    pay, ra, rb1, rb2, rcbuf, tsum, lsem, ssem, rsem,
):
    d = lax.axis_index("dom")
    q = lax.axis_index("col")
    x, z = d // NZ, d % NZ
    y, c = q // 2, q % 2
    sib = (d, q + 1 - 2 * c)

    def at_y(k):
        return (d, 2 * wrap(y + k, NY) + c)

    def at_xz(i, k):
        return (wrap(x + i, NX) * NZ + wrap(z + k, NZ), q)

    cols = [(d, wrap(q + k, N_COL)) for k in range(1, N_COL)]
    others = [(i, k) for i in range(NX) for k in range(NZ) if (i, k) != (0, 0)]
    partners = cols + [at_xz(i, k) for i, k in others]

    barrier = pltpu.get_barrier_semaphore()
    for partner in partners:
        pl.semaphore_signal(barrier, inc=1, device_id=partner, device_id_type=MESH)

    band_copy = pltpu.make_async_copy(band_hbm, tiles.at[pl.ds(0, TPD)], lsem.at[0])
    hub_copy = pltpu.make_async_copy(hub_hbm, tiles.at[pl.ds(TPD, HTD)], lsem.at[1])
    band_copy.start()
    hub_copy.start()
    state[0:K] = vec_in[...]
    state[K:] = dir_in[...]
    band_copy.wait()
    hub_copy.wait()

    def prepare(t, carry):
        high, low = split(tiles[t].T)
        weights[t, 0:TB] = high
        weights[t, TB:] = low
        return carry

    lax.fori_loop(0, NT, prepare, 0)
    pl.semaphore_wait(barrier, len(partners))

    def step(it, carry):
        counts = {"s": 0, "r": 0}

        def sems(n=1):
            s, r = counts["s"], counts["r"]
            counts["s"] += n
            counts["r"] += n
            return s

        def send(src, dst, sem, device):
            copy = pltpu.make_async_remote_copy(
                src_ref=src, dst_ref=dst, send_sem=ssem.at[it, sem], recv_sem=rsem.at[it, sem],
                device_id=device, device_id_type=MESH,
            )
            copy.start()
            return copy

        def arrived(ref, sem):
            pltpu.make_async_copy(ref, ref, rsem.at[it, sem]).wait()

        def sent(ref, sem):
            pltpu.make_async_copy(ref, ref, ssem.at[it, sem]).wait()

        pending = []

        pick = jnp.zeros((K, TB), F32)
        for j in range(OWN):
            block = state[0:K, TB * j : TB * (j + 1)]
            own[it, j] = block
            ext[it, HW + OWN * q + j] = block
            pick = pick + block * flt[2 * NT + j]
        cand[it] = pick

        g_ha = sems()
        for k in range(1, N_COL):
            peer = wrap(q + k, N_COL)
            send(cand.at[it, pl.ds(8 * peer, 8)], hca.at[it, q], g_ha, (d, peer))
        pending.append((hca.at[it, pl.ds(0, N_COL - 1)], g_ha))
        hca[it, q] = cand[it, pl.ds(8 * q, 8)]

        g_p = sems(NY)
        mine = ext.at[it, pl.ds(HW + OWN * q, OWN)]
        for k in (1, 3, 2):
            pending.append(send(own.at[it], mine, g_p + k, at_y(k)))
        pending.append(send(own.at[it], mine, g_p, sib))

        arrived(hca.at[it, pl.ds(0, N_COL - 1)], g_ha)
        piece = hca[it, 0]
        for k in range(1, N_COL):
            piece = piece + hca[it, k]
        hubx[it, d] = piece
        g_hb = sems()
        for i, k in others:
            send(hubx.at[it, d], hubx.at[it, d], g_hb, at_xz(i, k))
        pending.append((hubx.at[it, pl.ds(0, N_DOM - 1)], g_hb))

        g_pf = sems(NY)
        for k in (1, 3, 2):
            block = ext.at[it, pl.ds(HW + OWN * (2 * wrap(y - k, NY) + c), OWN)]
            arrived(block, g_p + k)
            pending.append(send(block, block, g_pf + k, sib))
        g_h = sems(4)
        low, high = pl.ds(OWN * c, OWN), pl.ds(HW + PB + OWN * c, OWN)
        pending.append(
            send(ext.at[it, pl.ds(HW + OWN * (N_COL - 2 + c), OWN)], ext.at[it, low], g_h, (wrap(d + 1, N_DOM), q))
        )
        pending.append(
            send(ext.at[it, pl.ds(HW + OWN * c, OWN)], ext.at[it, high], g_h + 1, (wrap(d - 1, N_DOM), q))
        )

        arrived(hubx.at[it, pl.ds(0, N_DOM - 1)], g_hb)
        g_c = sems(NY)
        mine = ext.at[it, pl.ds(EXT, HUBS), pl.ds(8 * q, 8)]
        for k in (1, 3, 2):
            pending.append(send(hubx.at[it], mine, g_c + k, at_y(k)))
        pending.append(send(hubx.at[it], mine, g_c, sib))
        for s in range(HUBS):
            ext[it, EXT + s, pl.ds(8 * q, 8)] = hubx[it, s]

        for n, part in enumerate((low, high)):
            arrived(ext.at[it, part], g_h + n)
            pending.append(send(ext.at[it, part], ext.at[it, part], g_h + 2 + n, sib))
        g_cf = sems(NY)
        for k in (1, 3, 2):
            part = ext.at[it, pl.ds(EXT, HUBS), pl.ds(8 * (2 * wrap(y - k, NY) + c), 8)]
            arrived(part, g_c + k)
            pending.append(send(part, part, g_cf + k, sib))
        other = 1 - c
        arrived(ext.at[it, pl.ds(HW + OWN * (2 * y + other), OWN)], g_p)
        for k in (1, 3, 2):
            arrived(ext.at[it, pl.ds(HW + OWN * (2 * wrap(y - k, NY) + other), OWN)], g_pf + k)
        arrived(ext.at[it, pl.ds(OWN * other, OWN)], g_h + 2)
        arrived(ext.at[it, pl.ds(HW + PB + OWN * other, OWN)], g_h + 3)
        arrived(ext.at[it, pl.ds(EXT, HUBS), pl.ds(8 * (2 * y + other), 8)], g_c)
        for k in (1, 3, 2):
            arrived(ext.at[it, pl.ds(EXT, HUBS), pl.ds(8 * (2 * wrap(y - k, NY) + other), 8)], g_cf + k)

        def products(g, total):
            for u in range(8):
                t = 8 * g + u
                high, low = split(ext[it, idx[NT + t]])
                left = jnp.concatenate(
                    [jnp.concatenate([high, high], axis=1), jnp.concatenate([low, jnp.zeros_like(low)], axis=1)], axis=0
                )
                both = jnp.dot(left, weights[idx[t]], preferred_element_type=F32)
                total = total * flt[t] + (both[:K] + both[K:])
                prods[t] = total
            return total

        lax.fori_loop(0, NT // 8, products, jnp.zeros((K, TB), F32))

        def partial(r):
            return prods[idx[2 * NT + r]] * flt[NT + r]

        g_s = sems(NY)
        for k in (1, 3, 2, 0):
            for j in range(OWN):
                ssend[k, j] = partial(OWN * (2 * wrap(y + k, NY) + other) + j)
            pending.append(send(ssend.at[k], srecv.at[it, k], g_s + k, sib))
        g_r = sems(NY)
        for k in (1, 3, 2):
            arrived(srecv.at[it, k], g_s + k)
            for j in range(OWN):
                rsum[k, j] = partial(OWN * (2 * wrap(y + k, NY) + c) + j) + srecv[it, k, j]
            pending.append(send(rsum.at[k], rrecv.at[it, k], g_r + k, at_y(k)))
        arrived(srecv.at[it, 0], g_s)
        for k in (1, 3, 2):
            arrived(rrecv.at[it, k], g_r + k)
        for j in range(OWN):
            summed = partial(OWN * q + j) + srecv[it, 0, j]
            for k in (1, 3, 2):
                summed = summed + rrecv[it, k, j]
            image[:, TB * j : TB * (j + 1)] = state[0:K, TB * j : TB * (j + 1)] - summed

        held = state[...]
        w = image[...]
        g0 = nt(held, held)
        pay[it, :, 0:128] = g0[:K]
        pay[it, :, 128:256] = g0[K:]
        pay[it, :, 256:384] = nt(w, held)
        pay[it, :, 384:512] = jnp.concatenate([nt(w, w), jnp.zeros((K, K), F32)], axis=1)
        g_a = sems()
        for k in range(1, N_COL):
            peer = wrap(q + k, N_COL)
            send(pay.at[it, pl.ds(8 * peer, 8)], ra.at[it, q], g_a, (d, peer))
        pending.append((ra.at[it, pl.ds(0, N_COL - 1)], g_a))
        ra[it, q] = pay[it, pl.ds(8 * q, 8)]
        arrived(ra.at[it, pl.ds(0, N_COL - 1)], g_a)
        total = ra[it, 0]
        for k in range(1, N_COL):
            total = total + ra[it, k]
        rb1[it, z] = total
        g_b = sems()
        for k in range(1, NZ):
            send(rb1.at[it, z], rb1.at[it, z], g_b, at_xz(0, k))
        pending.append((rb1.at[it, pl.ds(0, NZ - 1)], g_b))
        arrived(rb1.at[it, pl.ds(0, NZ - 1)], g_b)
        total = rb1[it, 0]
        for k in range(1, NZ):
            total = total + rb1[it, k]
        rb2[it, x] = total
        g_b2 = sems()
        for i in range(1, NX):
            send(rb2.at[it, x], rb2.at[it, x], g_b2, at_xz(i, 0))
        pending.append((rb2.at[it, pl.ds(0, NX - 1)], g_b2))
        arrived(rb2.at[it, pl.ds(0, NX - 1)], g_b2)
        total = rb2[it, 0]
        for k in range(1, NX):
            total = total + rb2[it, k]
        rcbuf[it, q] = total
        g_d = sems()
        for k in range(1, N_COL):
            send(rcbuf.at[it, q], rcbuf.at[it, q], g_d, (d, wrap(q + k, N_COL)))
        pending.append((rcbuf.at[it, pl.ds(0, N_COL - 1)], g_d))
        arrived(rcbuf.at[it, pl.ds(0, N_COL - 1)], g_d)
        moments = jnp.concatenate([rcbuf[it, k] for k in range(N_COL)], axis=0)
        gvd = jnp.concatenate([moments[:, 0:128], moments[:, 128:256]], axis=0)
        cross = moments[:, 256:384]
        ww = moments[:, 384 : 384 + K]
        ritz_t = cross[:, 0:K]
        ritz_out[...] = ritz_t.T

        coeff = rot[it]
        c1, c2, c3 = coeff[:, 0:K], coeff[:, K : 2 * K], coeff[:, 2 * K :]
        shift = nn(c2, ritz_t)
        yvd = jnp.concatenate([c1 - shift, c3], axis=1)
        zvd = jnp.concatenate([-shift, c3], axis=1)
        lower = jnp.concatenate([cross, ww], axis=1)
        yall = jnp.concatenate([yvd, c2], axis=1)
        kall = jnp.concatenate([nn(yall, jnp.concatenate([gvd, cross], axis=0)), nt(yall, lower)], axis=1)
        reduced = nt(kall, yall)
        inverse = eliminate(0.5 * (reduced + reduced.T))
        zall = jnp.concatenate([zvd, c2], axis=1)
        mix = jnp.concatenate([nn(inverse, yall), nn(inverse, zall)], axis=0)
        state[...] = nn(mix, jnp.concatenate([held, w], axis=0))

        for item in pending:
            if isinstance(item, tuple):
                sent(*item)
            else:
                item.wait_send()
        return carry

    lax.fori_loop(0, ITERS, step, 0)
    vec_out[...] = state[0:K]
    dir_out[...] = state[K:]


def plan(band_rows, band_cols, hub_rows, hub_slots, hub_blocks):
    rows = jnp.concatenate([band_rows, hub_rows])
    cols = jnp.concatenate([band_cols, EXT + hub_slots])
    at = jnp.arange(NT, dtype=jnp.int32)
    before = (rows[None, :] < rows[:, None]) | ((rows[None, :] == rows[:, None]) & (at[None, :] < at[:, None]))
    place = jnp.sum(before.astype(jnp.int32), axis=1)
    chosen = (place[None, :] == at[:, None]).astype(jnp.int32)
    order = jnp.sum(chosen * at[None, :], axis=1)
    ordered_cols = jnp.sum(chosen * cols[None, :], axis=1)
    ordered_rows = jnp.sum(chosen * rows[None, :], axis=1)
    keep = (ordered_rows == jnp.roll(ordered_rows, 1)) & (at > 0)
    upto = jnp.sum((rows[None, :] <= at[:, None]).astype(jnp.int32), axis=1)
    has = jnp.any(rows[None, :] == at[:, None], axis=1)
    last = jnp.maximum(upto - 1, 0)
    d, q = lax.axis_index("dom"), lax.axis_index("col")
    hub = hub_blocks[d] - d * PB - q * OWN == jnp.arange(OWN, dtype=jnp.int32)
    return jnp.concatenate([order, ordered_cols, last]), jnp.concatenate([keep, has, hub]).astype(F32)


def per_device(
    band_tiles, band_rows, band_cols, hub_tiles, hub_rows, hub_slots, hub_blocks,
    start_vectors, prior_directions, rotation,
):
    idx, flt = plan(band_rows, band_cols, hub_rows, hub_slots, hub_blocks)
    smem = pl.BlockSpec(memory_space=pltpu.SMEM)
    vmem = pl.BlockSpec(memory_space=pltpu.VMEM)
    anywhere = pl.BlockSpec(memory_space=pl.ANY)
    rows = K * 0 + 512
    vec, direc, ritz = pl.pallas_call(
        kernel,
        out_shape=(
            jax.ShapeDtypeStruct((K, rows), F32),
            jax.ShapeDtypeStruct((K, rows), F32),
            jax.ShapeDtypeStruct((K, K), F32),
        ),
        in_specs=[smem, smem, vmem, vmem, vmem, anywhere, anywhere],
        out_specs=(vmem, vmem, vmem),
        scratch_shapes=[
            pltpu.VMEM((NT, TB, TB), F32),
            pltpu.VMEM((NT, 2 * TB, TB), BF16),
            pltpu.VMEM((2 * K, rows), F32),
            pltpu.VMEM((K, rows), F32),
            pltpu.VMEM((ITERS, OWN, K, TB), F32),
            pltpu.VMEM((ITERS, EXT + HUBS, K, TB), F32),
            pltpu.VMEM((ITERS, K, TB), F32),
            pltpu.VMEM((ITERS, N_COL, 8, TB), F32),
            pltpu.VMEM((ITERS, N_DOM, 8, TB), F32),
            pltpu.VMEM((NT, K, TB), F32),
            pltpu.VMEM((NY, OWN, K, TB), F32),
            pltpu.VMEM((ITERS, NY, OWN, K, TB), F32),
            pltpu.VMEM((NY, OWN, K, TB), F32),
            pltpu.VMEM((ITERS, NY, OWN, K, TB), F32),
            pltpu.VMEM((ITERS, K, 512), F32),
            pltpu.VMEM((ITERS, N_COL, 8, 512), F32),
            pltpu.VMEM((ITERS, NZ, 8, 512), F32),
            pltpu.VMEM((ITERS, NX, 8, 512), F32),
            pltpu.VMEM((ITERS, N_COL, 8, 512), F32),
            pltpu.VMEM((8, 512), F32),
            pltpu.SemaphoreType.DMA((2,)),
            pltpu.SemaphoreType.DMA((ITERS, 40)),
            pltpu.SemaphoreType.DMA((ITERS, 40)),
        ],
        compiler_params=pltpu.CompilerParams(
            collective_id=0, has_side_effects=True, vmem_limit_bytes=48 * 1024 * 1024
        ),
        name="lobpcg",
    )(
        idx, flt, start_vectors.T, prior_directions.T, jnp.transpose(rotation, (0, 2, 1)),
        band_tiles, hub_tiles,
    )
    return vec.T, direc.T, ritz


def solution(mesh):
    return jax.shard_map(
        per_device,
        mesh=mesh,
        in_specs=(
            P(("dom", "col"), None, None),
            P(("dom", "col")),
            P(("dom", "col")),
            P(("dom", "col"), None, None),
            P(("dom", "col")),
            P(("dom", "col")),
            P(),
            P(("dom", "col"), None),
            P(("dom", "col"), None),
            P(),
        ),
        out_specs=(P(("dom", "col"), None), P(("dom", "col"), None), P()),
        check_vma=False,
    )
```

time: 1320 us -> 143 us (0.11)
  waiting for transfers between devices: 1050 us -> 0 us
  blocking collectives: 157 us -> 0 us
  Pallas kernels: 0 us -> 130 us
  matrix products: 28.8 us -> 0 us
  other arithmetic: 30.9 us -> 2.75 us
  between operations: 16 us -> 1.32 us
  local copies, waits for them, and re-layouts: 22.5 us -> 8.92 us
    psum x4 -> x0, waiting for transfers between devices: 937 us -> none  [the longest x2 483 us: per_device(): lax.psum(jnp.dot(basis.T, basis, precision=highest), ('dom', 'col'))]
    psum x2 -> x0, blocking collectives: 157 us -> none  [per_device(): lax.psum(jnp.dot(vectors.T, image, precision=highest), ('dom', 'col'))]
    pallas_call x0 -> x1, Pallas kernels: none -> 130 us  [per_device(): pl.pallas_call(kernel, out_shape=(jax.ShapeDtypeStruct((K, rows), F32), j...]
    reduce_scatter x2 -> x0, waiting for transfers between devices: 63.9 us -> none  [per_device(): lax.psum_scatter(partial_value.reshape(PB * TB, K), 'col', scatter_dimens...]
    all_gather x2 -> x0, waiting for transfers between devices: 51.3 us -> none  [per_device(): panel = lax.all_gather(vectors, 'col', axis=0, tiled=True)]
    dot_general x28 -> x0, matrix products: 28.3 us -> none  [the longest x2 6.29 us: per_device(): products = jnp.einsum('tij,tjc->tic', band_tiles, picked, precision=highest)]
    another operation x10 -> x0, other arithmetic: 24.1 us -> none  [the longest x6 13 us: rotate(): factor = jnp.linalg.cholesky(reduced)]
  transfers between devices with their start and end apart: 12 -> 0, of which waited for: 8 -> 0; matrix products, arithmetic and copies ran while one was open for 2% -> 0% of each run, Pallas kernels for 0% -> 0%
where the time goes in v1:
time: 143 us
  Pallas kernels  130 us (91%)
  local copies, waits for them, and re-layouts  8.92 us (6%)
  other arithmetic  2.75 us (2%)
    pallas_call x1, Pallas kernels, per_device(): pl.pallas_call(kernel, out_shape=(jax.ShapeDtypeStruct((K, rows), F32), j...  130 us
    unnamed x13, local copies, waits for them, and re-layouts  7.09 us

profile of v1, /device:TPU:1, one launch (start us, length us, event | category | flops | bytes accessed | tf_op | source)
XLA Modules:
  0.0 142.8 jit_solution(6076424365435513153)
XLA Ops:
  0.6 1.2 dynamic_slice.3
  2.5 0.7 broadcast_add_fusion
  3.2 0.8 pad_add_fusion
  4.0 0.2 convert_reduce_fusion.1
  4.1 0.1 fusion.2
  4.3 0.2 select_reduce_fusion
  4.4 0.6 slice.8
  5.0 0.7 compare_and_fusion
  5.7 0.1 add_convert_fusion.flt
  5.8 0.1 pad_add_fusion.2.idx
  5.9 0.0 copy-start
  5.9 1.4 copy-done
  7.3 0.0 copy-start.1
  7.3 1.0 copy-done.1
  8.3 0.0 copy-start.2
  8.3 0.9 copy-done.2
  9.3 0.0 copy-start.3
  9.3 0.9 copy-done.3
  10.2 0.0 copy-start.4
  10.2 0.9 copy-done.4
  11.1 129.8 %lobpcg.1 = (f32[64,512]{1,0:T(8,128)S(1)}, f32[64,512]{1,0:T(8,128)S(1)}, f32[64,64]{1,0:T(8,128)S(1)}) custom-call(s32[96]{0:T(128)S(1)} %pad_add_fusion.2.idx, f32[68]{0:T(128)S(1)} %add_convert_fusion.flt, f32[64,512]{1,0:T(8,128)S(1)} %bitcast.7, f32[64,512]{1,0:T(8,128)S(1)} %bitcast.8, f32[2,64,192]{2,1,0:T(8,128)S(1)} %bitcast.9, ...), custom_call_target="tpu_custom_call" | custom-call | tf_op jit(solution)/shard_map/lobpcg/pallas_call | solution.py:350
  140.9 0.7 copy.16
  141.6 0.7 copy.17
  142.2 0.6 copy.18
  (2 shorter events, 0.0 us)
Async XLA Ops:
  5.9 1.4 copy-start
  7.3 1.0 copy-start.1
  8.3 0.9 copy-start.2
  9.3 0.9 copy-start.3
  10.2 0.9 copy-start.4

commit v2 on v0

v2 whole, which is shorter than its diff:
```python
import jax
import jax.numpy as jnp
from jax import lax
from jax.experimental import pallas as pl
from jax.experimental.pallas import tpu as pltpu
from jax.sharding import PartitionSpec as P

TB = 128
K = 64
PB = 32
ITERS = 2
HW = 8
NZ = 8
NX = 4
NY = 4
N_DOM = 32
N_COL = 8
TPD = 24
HTD = 8
NT = TPD + HTD
OWN = 4
EXT = PB + 2 * HW
HUBS = 32
MESH = pl.DeviceIdType.MESH
F32 = jnp.float32
BF16 = jnp.bfloat16
HI = lax.Precision.HIGHEST


def wrap(value, count):
    return lax.rem(value + count, count)


def nn(a, b):
    return jnp.dot(a, b, precision=HI, preferred_element_type=F32)


def nt(a, b):
    return lax.dot_general(a, b, (((1,), (1,)), ((), ())), precision=HI, preferred_element_type=F32)


def split(value):
    high = value.astype(BF16)
    return high, (value - high.astype(F32)).astype(BF16)


def eliminate(matrix):
    full = (8, 2 * K)
    rows = lax.broadcasted_iota(jnp.int32, full, 0)
    lanes = lax.broadcasted_iota(jnp.int32, full, 1)
    wide = jnp.concatenate([matrix, jnp.zeros((K, K), F32)], axis=1)
    blocks = [jnp.where(lanes - K == rows + 8 * b, 1.0, wide[8 * b : 8 * b + 8]) for b in range(K // 8)]
    for home in range(K // 8):
        cols = [
            [jnp.broadcast_to(blocks[b][:, 8 * home + c : 8 * home + c + 1], full) for c in range(8)]
            for b in range(home, K // 8)
        ]
        work = [jnp.broadcast_to(blocks[home][r : r + 1, :], full) for r in range(8)]
        a = [[jnp.broadcast_to(cols[0][c][r : r + 1, :], full) for c in range(r + 1)] for r in range(8)]
        scale, done = [], []
        for c in range(8):
            scale.append(lax.rsqrt(a[c][c]))
            done.append(work[c] * scale[c])
            for r in range(c + 1, 8):
                a[r][c] = a[r][c] * scale[c]
            for r in range(c + 1, 8):
                for e in range(c + 1, r + 1):
                    a[r][e] = a[r][e] - a[r][c] * a[e][c]
                work[r] = work[r] - a[r][c] * done[c]
        back = [None] * 8
        for c in reversed(range(8)):
            value = done[c]
            for r in range(c + 1, 8):
                value = value - a[r][c] * back[r]
            back[c] = value * scale[c]
        for b in range(home + 1, K // 8):
            for c in range(8):
                blocks[b] = blocks[b] - cols[b - home][c] * back[c]
        for r in range(8):
            blocks[home] = jnp.where(rows == r, done[r], blocks[home])
    return jnp.concatenate(blocks, axis=0)[:, K:]


def plan(band_rows, band_cols, hub_rows, hub_slots):
    full = (NT, TB)
    sub = lax.broadcasted_iota(jnp.int32, full, 0)
    lane = lax.broadcasted_iota(jnp.int32, full, 1)
    key_s = jnp.zeros(full, jnp.int32)
    key_l = jnp.full(full, 4 * PB, jnp.int32)
    src_l = jnp.zeros(full, jnp.int32)
    for t in range(NT):
        key = band_rows[t] if t < TPD else PB + hub_rows[t - TPD]
        src = band_cols[t] if t < TPD else hub_slots[t - TPD]
        key_s = jnp.where(sub == t, key, key_s)
        key_l = jnp.where(lane == t, key, key_l)
        src_l = jnp.where(lane == t, src, src_l)

    def one(cond):
        return jnp.where(cond, 1, 0)

    same = jnp.where(sub < lane, one(key_s == key_l), 0)
    place = jnp.sum(one(key_s < key_l) + same, axis=0, keepdims=True)
    again = jnp.sum(same, axis=0, keepdims=True)
    place = jnp.where(lane < NT, jnp.broadcast_to(place, full), NT)
    chosen = one(place == sub)

    def across(value):
        return jnp.sum(value, axis=1, keepdims=True)

    columns = [
        across(chosen * lane),
        across(chosen * src_l),
        across(chosen * one(jnp.broadcast_to(again, full) > 0)),
        jnp.maximum(across(one(key_l <= sub)) - 1, 0),
        one(across(one(key_l == sub)) > 0),
        jnp.maximum(across(one(key_l <= sub + PB)) - 1, 0),
        one(across(one(key_l == sub + PB)) > 0),
    ]
    table = jnp.zeros(full, jnp.int32)
    for n, column in enumerate(columns):
        table = jnp.where(lane == n, jnp.broadcast_to(column, full), table)
    return table


def kernel(
    band_rows, band_cols, hub_rows, hub_slots, hub_blocks, vec_hbm, dir_hbm, rot_hbm, band_hbm, hub_hbm,
    vec_out, dir_out, ritz_out,
    tiles, weights, table_v, table, rot, xt, xt2,
    own, cand, hca, hubx, eb0, eb1, eb2, eh0, eh1, eh2, pr0, pr1, pr2,
    ssend, srecv, rsum, rrecv, pay, ra, rb1, rb2, rc, lsem, ssem, rsem,
):
    d = lax.axis_index("dom")
    q = lax.axis_index("col")
    x, z = d // NZ, d % NZ
    y, c = q // 2, q % 2
    other = 1 - c
    sib = (d, q + 1 - 2 * c)
    band, hub, prods = (eb0, eb1, eb2), (eh0, eh1, eh2), (pr0, pr1, pr2)

    def at_y(k):
        return (d, 2 * wrap(y + k, NY) + c)

    def at_xz(i, k):
        return (wrap(x + i, NX) * NZ + wrap(z + k, NZ), q)

    others = [(i, k) for i in range(NX) for k in range(NZ) if (i, k) != (0, 0)]
    partners = [(d, wrap(q + k, N_COL)) for k in range(1, N_COL)] + [at_xz(i, k) for i, k in others]

    local = []
    for n, (src, dst) in enumerate(
        (
            (vec_hbm, xt.at[pl.ds(0, K)]),
            (dir_hbm, xt.at[pl.ds(K, K)]),
            (band_hbm, tiles.at[pl.ds(0, TPD)]),
            (hub_hbm, tiles.at[pl.ds(TPD, HTD)]),
            (rot_hbm, rot),
        )
    ):
        local.append(pltpu.make_async_copy(src, dst, lsem.at[n]))
        local[n].start()
    barrier = pltpu.get_barrier_semaphore()
    for partner in partners:
        pl.semaphore_signal(barrier, inc=1, device_id=partner, device_id_type=MESH)

    counter = [0]
    pending = []

    def sems(n=1):
        counter[0] += n
        return counter[0] - n

    def send(src, dst, sem, device):
        copy = pltpu.make_async_remote_copy(
            src_ref=src, dst_ref=dst, send_sem=ssem.at[sem], recv_sem=rsem.at[sem],
            device_id=device, device_id_type=MESH,
        )
        copy.start()
        return copy

    def arrived(ref, sem):
        pltpu.make_async_copy(ref, ref, rsem.at[sem]).wait()

    def block_of(col):
        return pl.ds(HW + OWN * col, OWN)

    mask = [jnp.where(hub_blocks[d] - d * PB - q * OWN == j, 1.0, 0.0) for j in range(OWN)]
    names = ("ha", "p", "hb", "pf", "h", "hc", "hcf")
    gsem = [dict(zip(names, [sems(n) for n in (1, NY, 1, NY, 4, NY, NY)])) for _ in range(3)]

    def g_start(g, ref, first):
        pick = jnp.zeros((K, TB), F32)
        for j in range(OWN):
            block = ref[first : first + K, TB * j : TB * (j + 1)]
            own[g, j] = block
            band[g][HW + OWN * q + j] = block
            pick = pick + block * mask[j]
        cand[g] = pick
        for k in range(1, N_COL):
            peer = wrap(q + k, N_COL)
            send(cand.at[g, pl.ds(8 * peer, 8)], hca.at[g, q], gsem[g]["ha"], (d, peer))
        pending.append((hca.at[g, pl.ds(0, N_COL - 1)], gsem[g]["ha"]))
        hca[g, q] = cand[g, pl.ds(8 * q, 8)]
        mine = band[g].at[block_of(q)]
        for k in (2, 1, 3):
            pending.append(send(own.at[g], mine, gsem[g]["p"] + k, at_y(k)))
        pending.append(send(own.at[g], mine, gsem[g]["p"], sib))

    def g_hub(g):
        arrived(hca.at[g, pl.ds(0, N_COL - 1)], gsem[g]["ha"])
        piece = hca[g, 0]
        for k in range(1, N_COL):
            piece = piece + hca[g, k]
        hubx[g, d] = piece
        for i, k in sorted(others, key=lambda p: -min(p[0], NX - p[0]) - min(p[1], NZ - p[1])):
            send(hubx.at[g, d], hubx.at[g, d], gsem[g]["hb"], at_xz(i, k))
        pending.append((hubx.at[g, pl.ds(0, N_DOM - 1)], gsem[g]["hb"]))

    def g_panel(g):
        for k in (1, 3, 2):
            block = band[g].at[block_of(2 * wrap(y - k, NY) + c)]
            arrived(block, gsem[g]["p"] + k)
            pending.append(send(block, block, gsem[g]["pf"] + k, sib))
        low, high = band[g].at[pl.ds(OWN * c, OWN)], band[g].at[pl.ds(HW + PB + OWN * c, OWN)]
        pending.append(send(band[g].at[block_of(N_COL - 2 + c)], low, gsem[g]["h"], (wrap(d + 1, N_DOM), q)))
        pending.append(send(band[g].at[block_of(c)], high, gsem[g]["h"] + 1, (wrap(d - 1, N_DOM), q)))

    def g_spread(g):
        arrived(hubx.at[g, pl.ds(0, N_DOM - 1)], gsem[g]["hb"])
        mine = hub[g].at[pl.ds(0, HUBS), pl.ds(8 * q, 8)]
        for k in (2, 1, 3):
            pending.append(send(hubx.at[g], mine, gsem[g]["hc"] + k, at_y(k)))
        pending.append(send(hubx.at[g], mine, gsem[g]["hc"], sib))
        for s in range(HUBS):
            hub[g][s, pl.ds(8 * q, 8)] = hubx[g, s]

    def g_halo(g):
        for n, at in enumerate((OWN * c, HW + PB + OWN * c)):
            part = band[g].at[pl.ds(at, OWN)]
            arrived(part, gsem[g]["h"] + n)
            pending.append(send(part, part, gsem[g]["h"] + 2 + n, sib))

    def g_band_end(g):
        arrived(band[g].at[block_of(2 * y + other)], gsem[g]["p"])
        for k in (1, 3, 2):
            arrived(band[g].at[block_of(2 * wrap(y - k, NY) + other)], gsem[g]["pf"] + k)
        arrived(band[g].at[pl.ds(OWN * other, OWN)], gsem[g]["h"] + 2)
        arrived(band[g].at[pl.ds(HW + PB + OWN * other, OWN)], gsem[g]["h"] + 3)

    def g_pass(g):
        for k in (1, 3, 2):
            part = hub[g].at[pl.ds(0, HUBS), pl.ds(8 * (2 * wrap(y - k, NY) + c), 8)]
            arrived(part, gsem[g]["hc"] + k)
            pending.append(send(part, part, gsem[g]["hcf"] + k, sib))

    def g_hub_end(g):
        arrived(hub[g].at[pl.ds(0, HUBS), pl.ds(8 * (2 * y + other), 8)], gsem[g]["hc"])
        for k in (1, 3, 2):
            part = hub[g].at[pl.ds(0, HUBS), pl.ds(8 * (2 * wrap(y - k, NY) + other), 8)]
            arrived(part, gsem[g]["hcf"] + k)

    def multiply(g, source, first, count):
        def group(n, total):
            for u in range(8):
                t = first + 8 * n + u
                high, low = split(source[table[t, 1]])
                left = jnp.concatenate(
                    [jnp.concatenate([high, high], axis=1), jnp.concatenate([low, jnp.zeros_like(low)], axis=1)], axis=0
                )
                both = jnp.dot(left, weights[table[t, 0]], preferred_element_type=F32)
                total = total * table[t, 2].astype(F32) + (both[:K] + both[K:])
                prods[g][t] = total
            return total

        lax.fori_loop(0, count // 8, group, jnp.zeros((K, TB), F32))

    def row_sum(g, r):
        return prods[g][table[r, 3]] * table[r, 4].astype(F32) + prods[g][table[r, 5]] * table[r, 6].astype(F32)

    ssems = [(sems(NY), sems(NY)) for _ in range(ITERS)]

    def scatter_start(n, rows_of):
        for k in (2, 1, 3, 0):
            for j, block in enumerate(rows_of(OWN * (2 * wrap(y + k, NY) + other))):
                ssend[n, k, j] = block
            pending.append(send(ssend.at[n, k], srecv.at[n, k], ssems[n][0] + k, sib))
        for k in (2, 1, 3):
            blocks = rows_of(OWN * (2 * wrap(y + k, NY) + c))
            arrived(srecv.at[n, k], ssems[n][0] + k)
            for j, block in enumerate(blocks):
                rsum[n, k, j] = block + srecv[n, k, j]
            pending.append(send(rsum.at[n, k], rrecv.at[n, k], ssems[n][1] + k, at_y(k)))

    def scatter_end(n, rows_of):
        blocks = rows_of(OWN * q)
        arrived(srecv.at[n, 0], ssems[n][0])
        blocks = [block + srecv[n, 0, j] for j, block in enumerate(blocks)]
        for k in (1, 3, 2):
            arrived(rrecv.at[n, k], ssems[n][1] + k)
            blocks = [block + rrecv[n, k, j] for j, block in enumerate(blocks)]
        return jnp.concatenate(blocks, axis=1)

    asems = [sems(4) for _ in range(ITERS + 1)]

    def a_start(n):
        for k in range(1, N_COL):
            peer = wrap(q + k, N_COL)
            send(pay.at[n, pl.ds(8 * peer, 8)], ra.at[n, q], asems[n], (d, peer))
        pending.append((ra.at[n, pl.ds(0, N_COL - 1)], asems[n]))
        ra[n, q] = pay[n, pl.ds(8 * q, 8)]

    def a_sum(ref, n, count, sem):
        arrived(ref.at[n, pl.ds(0, count - 1)], sem)
        total = ref[n, 0]
        for k in range(1, count):
            total = total + ref[n, k]
        return total

    def a_z(n):
        rb1[n, z] = a_sum(ra, n, N_COL, asems[n])
        for k in (4, 3, 5, 2, 6, 1, 7):
            send(rb1.at[n, z], rb1.at[n, z], asems[n] + 1, at_xz(0, k))
        pending.append((rb1.at[n, pl.ds(0, NZ - 1)], asems[n] + 1))

    def a_x(n):
        rb2[n, x] = a_sum(rb1, n, NZ, asems[n] + 1)
        for i in (2, 1, 3):
            send(rb2.at[n, x], rb2.at[n, x], asems[n] + 2, at_xz(i, 0))
        pending.append((rb2.at[n, pl.ds(0, NX - 1)], asems[n] + 2))

    def a_back(n):
        rc[n, q] = a_sum(rb2, n, NX, asems[n] + 2)
        for k in range(1, N_COL):
            send(rc.at[n, q], rc.at[n, q], asems[n] + 3, (d, wrap(q + k, N_COL)))
        pending.append((rc.at[n, pl.ds(0, N_COL - 1)], asems[n] + 3))

    def a_end(n):
        arrived(rc.at[n, pl.ds(0, N_COL - 1)], asems[n] + 3)
        return jnp.concatenate([rc[n, k] for k in range(N_COL)], axis=0)

    def moments(ref):
        return jnp.concatenate([nt(ref[2 * K :], ref[...]), jnp.zeros((K, K), F32)], axis=1)

    def coefficients(it, gvd, sums):
        lower = sums[:, : 3 * K]
        cross = sums[:, : 2 * K]
        ritz_t = sums[:, :K]
        coeff = rot[it]
        c1, c2, c3 = coeff[:, 0:K], coeff[:, K : 2 * K], coeff[:, 2 * K :]
        shift = nn(c2, ritz_t)
        yall = jnp.concatenate([c1 - shift, c3, c2], axis=1)
        zall = jnp.concatenate([-shift, c3, c2], axis=1)
        upper = jnp.concatenate([gvd, cross], axis=0)
        kall = jnp.concatenate([nn(yall, upper), nt(yall, lower)], axis=1)
        reduced = nt(kall, yall)
        inverse = eliminate(0.5 * (reduced + reduced.T))
        return jnp.concatenate([nn(inverse, yall), nn(inverse, zall)], axis=0), upper, lower

    local[0].wait()
    pl.semaphore_wait(barrier, len(partners))
    g_start(0, xt, 0)
    local[1].wait()
    both = xt[0 : 2 * K, :]
    gram = nt(both, both)
    pay[0] = jnp.concatenate([gram[:K], gram[K:]], axis=1)
    a_start(0)
    table_v[...] = plan(band_rows, band_cols, hub_rows, hub_slots)
    to_smem = pltpu.make_async_copy(table_v, table, lsem.at[5])
    to_smem.start()
    g_hub(0)
    for n in (2, 3, 4):
        local[n].wait()

    def prepare(t, carry):
        high, low = split(tiles[t].T)
        weights[t, 0:TB] = high
        weights[t, TB:] = low
        return carry

    lax.fori_loop(0, NT // 2, prepare, 0)
    a_z(0)
    lax.fori_loop(NT // 2, NT, prepare, 0)
    to_smem.wait()
    g_panel(0)
    g_spread(0)
    g_halo(0)
    g_band_end(0)
    multiply(0, band[0], 0, TPD)
    g_pass(0)
    g_start(1, xt, K)
    g_hub_end(0)
    multiply(0, hub[0], TPD, HTD)
    a_x(0)
    g_hub(1)

    def first_rows(r):
        return [row_sum(0, r + j) for j in range(OWN)]

    scatter_start(0, first_rows)
    a_back(0)
    g_panel(1)
    xt[2 * K :] = xt[0:K] - scatter_end(0, first_rows)
    pay[1] = moments(xt)
    a_start(1)
    g_start(2, xt, 2 * K)
    sums0 = a_end(0)
    gvd = jnp.concatenate([sums0[:, : 2 * K], sums0[:, 2 * K :]], axis=0)
    g_spread(1)
    g_halo(1)
    a_z(1)
    g_hub(2)
    g_band_end(1)
    multiply(1, band[1], 0, TPD)
    a_x(1)
    g_panel(2)
    g_pass(1)
    a_back(1)
    g_spread(2)
    g_halo(2)
    g_hub_end(1)
    multiply(1, hub[1], TPD, HTD)
    g_band_end(2)
    multiply(2, band[2], 0, TPD)
    sums1 = a_end(1)
    mix, upper, lower = coefficients(0, gvd, sums1)
    g_pass(2)
    mix_high, mix_low = split(mix[:K])
    mix_both = jnp.concatenate([mix_high, mix_low], axis=0)
    xt2[0 : 2 * K] = nn(mix, xt[...])
    carried = jnp.concatenate([nn(mix, upper), nt(mix, lower)], axis=1)
    gvd = nt(carried, mix)
    g_hub_end(2)
    multiply(2, hub[2], TPD, HTD)

    def second_rows(r):
        stack = jnp.concatenate(
            [jnp.concatenate([row_sum(g, r + j) for j in range(OWN)], axis=1) for g in range(3)], axis=0
        )
        high, low = split(stack)
        one = jnp.dot(mix_both, high, preferred_element_type=F32)
        two = jnp.dot(mix_high, low, preferred_element_type=F32)
        out = one[:K] + one[K:] + two
        return [out[:, TB * j : TB * (j + 1)] for j in range(OWN)]

    scatter_start(1, second_rows)
    xt2[2 * K :] = xt2[0:K] - scatter_end(1, second_rows)
    pay[2] = moments(xt2)
    a_start(2)
    a_z(2)
    a_x(2)
    a_back(2)
    sums2 = a_end(2)
    ritz_out[...] = sums2[:, :K].T
    mix2, _, _ = coefficients(1, gvd, sums2)
    final = nn(mix2, xt2[...])
    vec_out[...] = final[:K]
    dir_out[...] = final[K:]

    for item in pending:
        if isinstance(item, tuple):
            ref, sem = item
            pltpu.make_async_copy(ref, ref, ssem.at[sem]).wait()
        else:
            item.wait_send()


def per_device(
    band_tiles, band_rows, band_cols, hub_tiles, hub_rows, hub_slots, hub_blocks,
    start_vectors, prior_directions, rotation,
):
    smem = pl.BlockSpec(memory_space=pltpu.SMEM)
    vmem = pl.BlockSpec(memory_space=pltpu.VMEM)
    hbm = pl.BlockSpec(memory_space=pltpu.HBM)
    rows = start_vectors.shape[0]
    ext = [pltpu.VMEM((EXT, K, TB), F32)] * 3 + [pltpu.VMEM((HUBS, K, TB), F32)] * 3
    vec, direc, ritz = pl.pallas_call(
        kernel,
        out_shape=(
            jax.ShapeDtypeStruct((K, rows), F32),
            jax.ShapeDtypeStruct((K, rows), F32),
            jax.ShapeDtypeStruct((K, K), F32),
        ),
        in_specs=[smem] * 5 + [hbm] * 5,
        out_specs=(vmem, vmem, vmem),
        scratch_shapes=[
            pltpu.VMEM((NT, TB, TB), F32),
            pltpu.VMEM((NT, 2 * TB, TB), BF16),
            pltpu.VMEM((NT, TB), jnp.int32),
            pltpu.SMEM((NT, TB), jnp.int32),
            pltpu.VMEM((ITERS, K, 3 * K), F32),
            pltpu.VMEM((3 * K, rows), F32),
            pltpu.VMEM((3 * K, rows), F32),
            pltpu.VMEM((3, OWN, K, TB), F32),
            pltpu.VMEM((3, K, TB), F32),
            pltpu.VMEM((3, N_COL, 8, TB), F32),
            pltpu.VMEM((3, N_DOM, 8, TB), F32),
            *ext,
            *[pltpu.VMEM((NT, K, TB), F32)] * 3,
            pltpu.VMEM((ITERS, NY, OWN, K, TB), F32),
            pltpu.VMEM((ITERS, NY, OWN, K, TB), F32),
            pltpu.VMEM((ITERS, NY, OWN, K, TB), F32),
            pltpu.VMEM((ITERS, NY, OWN, K, TB), F32),
            pltpu.VMEM((ITERS + 1, K, 4 * K), F32),
            pltpu.VMEM((ITERS + 1, N_COL, 8, 4 * K), F32),
            pltpu.VMEM((ITERS + 1, NZ, 8, 4 * K), F32),
            pltpu.VMEM((ITERS + 1, NX, 8, 4 * K), F32),
            pltpu.VMEM((ITERS + 1, N_COL, 8, 4 * K), F32),
            pltpu.SemaphoreType.DMA((6,)),
            pltpu.SemaphoreType.DMA((100,)),
            pltpu.SemaphoreType.DMA((100,)),
        ],
        compiler_params=pltpu.CompilerParams(
            collective_id=0, has_side_effects=True, vmem_limit_bytes=56 * 1024 * 1024
        ),
        name="lobpcg",
    )(
        band_rows, band_cols, hub_rows, hub_slots, hub_blocks, start_vectors.T, prior_directions.T,
        jnp.transpose(rotation, (0, 2, 1)), band_tiles, hub_tiles,
    )
    return vec.T, direc.T, ritz


def solution(mesh):
    return jax.shard_map(
        per_device,
        mesh=mesh,
        in_specs=(
            P(("dom", "col"), None, None),
            P(("dom", "col")),
            P(("dom", "col")),
            P(("dom", "col"), None, None),
            P(("dom", "col")),
            P(("dom", "col")),
            P(),
            P(("dom", "col"), None),
            P(("dom", "col"), None),
            P(),
        ),
        out_specs=(P(("dom", "col"), None), P(("dom", "col"), None), P()),
        check_vma=False,
    )
```

time: 1320 us -> 108 us (0.08)
  waiting for transfers between devices: 1050 us -> 0 us
  blocking collectives: 157 us -> 0 us
  Pallas kernels: 0 us -> 103 us
  other arithmetic: 30.9 us -> 0 us
  matrix products: 28.8 us -> 0 us
  local copies, waits for them, and re-layouts: 22.5 us -> 4.51 us
  between operations: 16 us -> 0.64 us
    psum x4 -> x0, waiting for transfers between devices: 937 us -> none  [the longest x2 483 us: per_device(): lax.psum(jnp.dot(basis.T, basis, precision=highest), ('dom', 'col'))]
    psum x2 -> x0, blocking collectives: 157 us -> none  [per_device(): lax.psum(jnp.dot(vectors.T, image, precision=highest), ('dom', 'col'))]
    pallas_call x0 -> x1, Pallas kernels: none -> 103 us  [per_device(): pl.pallas_call(kernel, out_shape=(jax.ShapeDtypeStruct((K, rows), F32), j...]
    reduce_scatter x2 -> x0, waiting for transfers between devices: 63.9 us -> none  [per_device(): lax.psum_scatter(partial_value.reshape(PB * TB, K), 'col', scatter_dimens...]
    all_gather x2 -> x0, waiting for transfers between devices: 51.3 us -> none  [per_device(): panel = lax.all_gather(vectors, 'col', axis=0, tiled=True)]
    dot_general x28 -> x0, matrix products: 28.3 us -> none  [the longest x2 6.29 us: per_device(): products = jnp.einsum('tij,tjc->tic', band_tiles, picked, precision=highest)]
    another operation x10 -> x0, other arithmetic: 24.1 us -> none  [the longest x6 13 us: rotate(): factor = jnp.linalg.cholesky(reduced)]
  transfers between devices with their start and end apart: 12 -> 0, of which waited for: 8 -> 0; matrix products, arithmetic and copies ran while one was open for 2% -> 0% of each run, Pallas kernels for 0% -> 0%
where the time goes in v2:
time: 108 us
  Pallas kernels  103 us (95%)
  local copies, waits for them, and re-layouts  4.51 us (4%)
    pallas_call x1, Pallas kernels, per_device(): pl.pallas_call(kernel, out_shape=(jax.ShapeDtypeStruct((K, rows), F32), j...  103 us
    unnamed x3, local copies, waits for them, and re-layouts  4.51 us

profile of v2, /device:TPU:1, one launch (start us, length us, event | category | flops | bytes accessed | tf_op | source)
XLA Modules:
  0.0 108.0 jit_solution(7022001601498562869)
XLA Ops:
  0.6 102.8 %lobpcg.1 = (f32[64,512]{1,0:T(8,128)}, f32[64,512]{1,0:T(8,128)}, f32[64,64]{1,0:T(8,128)}) custom-call(s32[24]{0:T(128)} %band_rows.1, s32[24]{0:T(128)} %band_cols.1, s32[8]{0:T(128)} %hub_rows.1, s32[8]{0:T(128)} %hub_slots.1, s32[32]{0:T(128)} %hub_blocks.1, f32[64,512]{1,0:T(8,128)} %bitcast.5, f32[64,512]{1,0:T(8,128)} %bitcast.6, ...), custom_call_target="tpu_custom_call" | custom-call | tf_op jit(solution)/shard_map/lobpcg/pallas_call | solution.py:475
  103.5 1.6 %copy.16 = f32[512,64]{0,1:T(8,128)} copy(f32[512,64]{0,1:T(8,128)} %bitcast.9) | data formatting | bytes 262144
  105.0 1.6 %copy.17 = f32[512,64]{0,1:T(8,128)} copy(f32[512,64]{0,1:T(8,128)} %bitcast.8) | data formatting | bytes 262144
  106.6 1.4 %copy.18 = f32[64,64]{1,0:T(8,128)} copy(f32[64,64]{1,0:T(8,128)} %get-tuple-element.14) | data formatting | bytes 32768

commit v3 on v2

--- a/solution.py
+++ b/solution.py
@@ -21,6 +21,7 @@
 OWN = 4
 EXT = PB + 2 * HW
 HUBS = 32
+HALF = 32
 MESH = pl.DeviceIdType.MESH
 F32 = jnp.float32
 BF16 = jnp.bfloat16
@@ -124,10 +125,11 @@
 
 def kernel(
     band_rows, band_cols, hub_rows, hub_slots, hub_blocks, vec_hbm, dir_hbm, rot_hbm, band_hbm, hub_hbm,
-    vec_out, dir_out, ritz_out,
-    tiles, weights, table_v, table, rot, xt, xt2,
-    own, cand, hca, hubx, eb0, eb1, eb2, eh0, eh1, eh2, pr0, pr1, pr2,
-    ssend, srecv, rsum, rrecv, pay, ra, rb1, rb2, rc, lsem, ssem, rsem,
+    mix_out, xt2, ritz_out,
+    tiles, weights, table_v, table, rot, xt,
+    own, cand, hca, hubz, eb0, eb1, eb2, eh0, eh1, eh2, pr0, pr1, pr2, mixed,
+    ssend, srecv, rsum, rrecv, pay0, ra0, rb0, rx0, rc0, pay1, ra1, rb1, rx1, rc1,
+    wpay, wrecv, wplane, wz, wend, lsem, ssem, rsem,
 ):
     d = lax.axis_index("dom")
     q = lax.axis_index("col")
@@ -185,35 +187,42 @@
 
     mask = [jnp.where(hub_blocks[d] - d * PB - q * OWN == j, 1.0, 0.0) for j in range(OWN)]
     names = ("ha", "p", "hb", "pf", "h", "hc", "hcf")
-    gsem = [dict(zip(names, [sems(n) for n in (1, NY, 1, NY, 4, NY, NY)])) for _ in range(3)]
+    gsem = [dict(zip(names, [sems(n) for n in (1, NY, 1, NY, 4, NX, NX)])) for _ in range(3)]
+    hub_row = jnp.clip(hub_blocks[d] - d * PB, 0, PB - 1)
 
     def g_start(g, ref, first):
-        pick = jnp.zeros((K, TB), F32)
         for j in range(OWN):
             block = ref[first : first + K, TB * j : TB * (j + 1)]
             own[g, j] = block
             band[g][HW + OWN * q + j] = block
-            pick = pick + block * mask[j]
-        cand[g] = pick
-        for k in range(1, N_COL):
-            peer = wrap(q + k, N_COL)
-            send(cand.at[g, pl.ds(8 * peer, 8)], hca.at[g, q], gsem[g]["ha"], (d, peer))
-        pending.append((hca.at[g, pl.ds(0, N_COL - 1)], gsem[g]["ha"]))
-        hca[g, q] = cand[g, pl.ds(8 * q, 8)]
         mine = band[g].at[block_of(q)]
         for k in (2, 1, 3):
             pending.append(send(own.at[g], mine, gsem[g]["p"] + k, at_y(k)))
         pending.append(send(own.at[g], mine, gsem[g]["p"], sib))
 
-    def g_hub(g):
+    def masked(ref, first):
+        pick = jnp.zeros((K, TB), F32)
+        for j in range(OWN):
+            pick = pick + ref[first : first + K, TB * j : TB * (j + 1)] * mask[j]
+        return pick
+
+    def g_hub_start(g, term):
+        cand[g] = term
+        for k in range(1, N_COL):
+            peer = wrap(q + k, N_COL)
+            send(cand.at[g, pl.ds(HALF * (peer % 2), HALF)], hca.at[g, q], gsem[g]["ha"], (d, peer))
+        pending.append((hca.at[g, pl.ds(0, N_COL - 1)], gsem[g]["ha"]))
+        hca[g, q] = cand[g, pl.ds(HALF * c, HALF)]
+
+    def g_hub(g, base=None):
         arrived(hca.at[g, pl.ds(0, N_COL - 1)], gsem[g]["ha"])
         piece = hca[g, 0]
         for k in range(1, N_COL):
             piece = piece + hca[g, k]
-        hubx[g, d] = piece
-        for i, k in sorted(others, key=lambda p: -min(p[0], NX - p[0]) - min(p[1], NZ - p[1])):
-            send(hubx.at[g, d], hubx.at[g, d], gsem[g]["hb"], at_xz(i, k))
-        pending.append((hubx.at[g, pl.ds(0, N_DOM - 1)], gsem[g]["hb"]))
+        hubz[g, z] = piece if base is None else base - piece
+        for k in (4, 3, 5, 2, 6, 1, 7):
+            send(hubz.at[g, z], hubz.at[g, z], gsem[g]["hb"], at_xz(0, k))
+        pending.append((hubz.at[g, pl.ds(0, NZ - 1)], gsem[g]["hb"]))
 
     def g_panel(g):
         for k in (1, 3, 2):
@@ -224,14 +233,17 @@
         pending.append(send(band[g].at[block_of(N_COL - 2 + c)], low, gsem[g]["h"], (wrap(d + 1, N_DOM), q)))
         pending.append(send(band[g].at[block_of(c)], high, gsem[g]["h"] + 1, (wrap(d - 1, N_DOM), q)))
 
+    def slab(g, at_x, half):
+        return hub[g].at[pl.ds(NZ * at_x, NZ), pl.ds(HALF * half, HALF)]
+
     def g_spread(g):
-        arrived(hubx.at[g, pl.ds(0, N_DOM - 1)], gsem[g]["hb"])
-        mine = hub[g].at[pl.ds(0, HUBS), pl.ds(8 * q, 8)]
-        for k in (2, 1, 3):
-            pending.append(send(hubx.at[g], mine, gsem[g]["hc"] + k, at_y(k)))
-        pending.append(send(hubx.at[g], mine, gsem[g]["hc"], sib))
-        for s in range(HUBS):
-            hub[g][s, pl.ds(8 * q, 8)] = hubx[g, s]
+        arrived(hubz.at[g, pl.ds(0, NZ - 1)], gsem[g]["hb"])
+        mine = slab(g, x, c)
+        for i in (2, 1, 3):
+            pending.append(send(hubz.at[g], mine, gsem[g]["hc"] + i, at_xz(i, 0)))
+        pending.append(send(hubz.at[g], mine, gsem[g]["hcf"], sib))
+        for s in range(NZ):
+            hub[g][NZ * x + s, pl.ds(HALF * c, HALF)] = hubz[g, s]
 
     def g_halo(g):
         for n, at in enumerate((OWN * c, HW + PB + OWN * c)):
@@ -239,24 +251,24 @@
             arrived(part, gsem[g]["h"] + n)
             pending.append(send(part, part, gsem[g]["h"] + 2 + n, sib))
 
-    def g_band_end(g):
+    def g_panel_end(g):
         arrived(band[g].at[block_of(2 * y + other)], gsem[g]["p"])
         for k in (1, 3, 2):
             arrived(band[g].at[block_of(2 * wrap(y - k, NY) + other)], gsem[g]["pf"] + k)
+
+    def g_halo_end(g):
         arrived(band[g].at[pl.ds(OWN * other, OWN)], gsem[g]["h"] + 2)
         arrived(band[g].at[pl.ds(HW + PB + OWN * other, OWN)], gsem[g]["h"] + 3)
 
     def g_pass(g):
-        for k in (1, 3, 2):
-            part = hub[g].at[pl.ds(0, HUBS), pl.ds(8 * (2 * wrap(y - k, NY) + c), 8)]
-            arrived(part, gsem[g]["hc"] + k)
-            pending.append(send(part, part, gsem[g]["hcf"] + k, sib))
+        for i in (1, 3, 2):
+            part = slab(g, wrap(x - i, NX), c)
+            arrived(part, gsem[g]["hc"] + i)
+            pending.append(send(part, part, gsem[g]["hcf"] + i, sib))
 
     def g_hub_end(g):
-        arrived(hub[g].at[pl.ds(0, HUBS), pl.ds(8 * (2 * y + other), 8)], gsem[g]["hc"])
-        for k in (1, 3, 2):
-            part = hub[g].at[pl.ds(0, HUBS), pl.ds(8 * (2 * wrap(y - k, NY) + other), 8)]
-            arrived(part, gsem[g]["hcf"] + k)
+        for i in (0, 1, 3, 2):
+            arrived(slab(g, wrap(x - i, NX), other), gsem[g]["hcf"] + i)
 
     def multiply(g, source, first, count):
         def group(n, total):
@@ -289,9 +301,9 @@
             for j, block in enumerate(blocks):
                 rsum[n, k, j] = block + srecv[n, k, j]
             pending.append(send(rsum.at[n, k], rrecv.at[n, k], ssems[n][1] + k, at_y(k)))
-
-    def scatter_end(n, rows_of):
-        blocks = rows_of(OWN * q)
+        return rows_of(OWN * q)
+
+    def scatter_end(n, blocks):
         arrived(srecv.at[n, 0], ssems[n][0])
         blocks = [block + srecv[n, 0, j] for j, block in enumerate(blocks)]
         for k in (1, 3, 2):
@@ -299,76 +311,113 @@
             blocks = [block + rrecv[n, k, j] for j, block in enumerate(blocks)]
         return jnp.concatenate(blocks, axis=1)
 
+    def panel_cross(block_at, groups):
+        def some(n, total):
+            for u in range(4):
+                r = 4 * n + u
+                ph, pl_ = split(block_at(r))
+                gh, gl = split(jnp.concatenate([band[g][HW + r] for g in groups], axis=0))
+                total = total + lax.dot_general(
+                    jnp.concatenate([ph, ph, pl_], axis=1), jnp.concatenate([gh, gl, gh], axis=1),
+                    (((1,), (1,)), ((), ())), preferred_element_type=F32,
+                )
+            return total
+
+        return lax.fori_loop(0, PB // 4, some, jnp.zeros((K, K * len(groups)), F32))
+
+    sets = ((pay0, ra0, rb0, rx0, rc0), (pay1, ra1, rb1, rx1, rc1))
     asems = [sems(4) for _ in range(ITERS + 1)]
 
-    def a_start(n):
+    def refs(n):
+        return [(ref.at[0] if n == 0 else ref.at[n - 1]) for ref in sets[min(n, 1)]]
+
+    def a_start(n, value):
+        pay, ra, _, _, _ = refs(n)
+        pay[...] = value
         for k in range(1, N_COL):
             peer = wrap(q + k, N_COL)
-            send(pay.at[n, pl.ds(8 * peer, 8)], ra.at[n, q], asems[n], (d, peer))
-        pending.append((ra.at[n, pl.ds(0, N_COL - 1)], asems[n]))
-        ra[n, q] = pay[n, pl.ds(8 * q, 8)]
-
-    def a_sum(ref, n, count, sem):
-        arrived(ref.at[n, pl.ds(0, count - 1)], sem)
-        total = ref[n, 0]
+            send(pay.at[pl.ds(8 * peer, 8)], ra.at[q], asems[n], (d, peer))
+        pending.append((ra.at[pl.ds(0, N_COL - 1)], asems[n]))
+        ra[q] = pay[pl.ds(8 * q, 8)]
+
+    def a_sum(ref, count, sem):
+        arrived(ref.at[pl.ds(0, count - 1)], sem)
+        total = ref[0]
         for k in range(1, count):
-            total = total + ref[n, k]
+            total = total + ref[k]
         return total
 
     def a_z(n):
-        rb1[n, z] = a_sum(ra, n, N_COL, asems[n])
+        _, ra, rb, _, _ = refs(n)
+        rb[z] = a_sum(ra, N_COL, asems[n])
         for k in (4, 3, 5, 2, 6, 1, 7):
-            send(rb1.at[n, z], rb1.at[n, z], asems[n] + 1, at_xz(0, k))
-        pending.append((rb1.at[n, pl.ds(0, NZ - 1)], asems[n] + 1))
+            send(rb.at[z], rb.at[z], asems[n] + 1, at_xz(0, k))
+        pending.append((rb.at[pl.ds(0, NZ - 1)], asems[n] + 1))
 
     def a_x(n):
-        rb2[n, x] = a_sum(rb1, n, NZ, asems[n] + 1)
+        _, _, rb, rx, _ = refs(n)
+        rx[x] = a_sum(rb, NZ, asems[n] + 1)
         for i in (2, 1, 3):
-            send(rb2.at[n, x], rb2.at[n, x], asems[n] + 2, at_xz(i, 0))
-        pending.append((rb2.at[n, pl.ds(0, NX - 1)], asems[n] + 2))
+            send(rx.at[x], rx.at[x], asems[n] + 2, at_xz(i, 0))
+        pending.append((rx.at[pl.ds(0, NX - 1)], asems[n] + 2))
 
     def a_back(n):
-        rc[n, q] = a_sum(rb2, n, NX, asems[n] + 2)
+        _, _, _, rx, rc = refs(n)
+        rc[q] = a_sum(rx, NX, asems[n] + 2)
         for k in range(1, N_COL):
-            send(rc.at[n, q], rc.at[n, q], asems[n] + 3, (d, wrap(q + k, N_COL)))
-        pending.append((rc.at[n, pl.ds(0, N_COL - 1)], asems[n] + 3))
+            send(rc.at[q], rc.at[q], asems[n] + 3, (d, wrap(q + k, N_COL)))
+        pending.append((rc.at[pl.ds(0, N_COL - 1)], asems[n] + 3))
 
     def a_end(n):
-        arrived(rc.at[n, pl.ds(0, N_COL - 1)], asems[n] + 3)
-        return jnp.concatenate([rc[n, k] for k in range(N_COL)], axis=0)
-
-    def moments(ref):
-        return jnp.concatenate([nt(ref[2 * K :], ref[...]), jnp.zeros((K, K), F32)], axis=1)
-
-    def coefficients(it, gvd, sums):
-        lower = sums[:, : 3 * K]
-        cross = sums[:, : 2 * K]
-        ritz_t = sums[:, :K]
+        _, _, _, _, rc = refs(n)
+        arrived(rc.at[pl.ds(0, N_COL - 1)], asems[n] + 3)
+        return jnp.concatenate([rc[k] for k in range(N_COL)], axis=0)
+
+    wsems = [sems(4) for _ in range(ITERS)]
+
+    def w_start(n, w):
+        square = nt(w, w)
+        wpay[n] = jnp.concatenate([square[: K // 2], square[K // 2 :]], axis=1)
+        pending.append(send(wpay.at[n, pl.ds(16 * other, 16)], wrecv.at[n], wsems[n], sib))
+
+    def w_plane(n):
+        arrived(wrecv.at[n], wsems[n])
+        at = x * NY + y
+        wplane[n, at] = wpay[n, pl.ds(16 * c, 16)] + wrecv[n]
+        for i, k in ((2, 2), (2, 1), (2, 3), (1, 2), (3, 2), (2, 0), (0, 2), (1, 1), (1, 3), (3, 1), (3, 3), (1, 0), (3, 0), (0, 1), (0, 3)):
+            peer = (wrap(x + i, NX) * NZ + z, 2 * wrap(y + k, NY) + c)
+            send(wplane.at[n, at], wplane.at[n, at], wsems[n] + 1, peer)
+        pending.append((wplane.at[n, pl.ds(0, NX * NY - 1)], wsems[n] + 1))
+
+    def w_z(n):
+        wz[n, z] = a_sum(wplane.at[n], NX * NY, wsems[n] + 1)
+        for k in (4, 3, 5, 2, 6, 1, 7):
+            send(wz.at[n, z], wz.at[n, z], wsems[n] + 2, at_xz(0, k))
+        pending.append((wz.at[n, pl.ds(0, NZ - 1)], wsems[n] + 2))
+
+    def w_back(n):
+        wend[n, pl.ds(16 * c, 16)] = a_sum(wz.at[n], NZ, wsems[n] + 2)
+        half = wend.at[n, pl.ds(16 * c, 16)]
+        pending.append(send(half, half, wsems[n] + 3, sib))
+
+    def w_end(n):
+        arrived(wend.at[n, pl.ds(16 * other, 16)], wsems[n] + 3)
+        whole = wend[n]
+        return jnp.concatenate([whole[:, :K], whole[:, K:]], axis=0)
+
+    def prepared(it, gvd, cross):
         coeff = rot[it]
         c1, c2, c3 = coeff[:, 0:K], coeff[:, K : 2 * K], coeff[:, 2 * K :]
-        shift = nn(c2, ritz_t)
+        shift = nn(c2, cross[:, :K])
         yall = jnp.concatenate([c1 - shift, c3, c2], axis=1)
         zall = jnp.concatenate([-shift, c3, c2], axis=1)
         upper = jnp.concatenate([gvd, cross], axis=0)
-        kall = jnp.concatenate([nn(yall, upper), nt(yall, lower)], axis=1)
-        reduced = nt(kall, yall)
-        inverse = eliminate(0.5 * (reduced + reduced.T))
-        return jnp.concatenate([nn(inverse, yall), nn(inverse, zall)], axis=0), upper, lower
-
-    local[0].wait()
-    pl.semaphore_wait(barrier, len(partners))
-    g_start(0, xt, 0)
-    local[1].wait()
-    both = xt[0 : 2 * K, :]
-    gram = nt(both, both)
-    pay[0] = jnp.concatenate([gram[:K], gram[K:]], axis=1)
-    a_start(0)
-    table_v[...] = plan(band_rows, band_cols, hub_rows, hub_slots)
-    to_smem = pltpu.make_async_copy(table_v, table, lsem.at[5])
-    to_smem.start()
-    g_hub(0)
-    for n in (2, 3, 4):
-        local[n].wait()
+        return yall, zall, upper, nn(yall, upper)
+
+    def coefficients(yall, zall, left, lower):
+        reduced = nt(jnp.concatenate([left, nt(yall, lower)], axis=1), yall)
+        inverse = eliminate(reduced)
+        return jnp.concatenate([nn(inverse, yall), nn(inverse, zall)], axis=0)
 
     def prepare(t, carry):
         high, low = split(tiles[t].T)
@@ -376,58 +425,85 @@
         weights[t, TB:] = low
         return carry
 
-    lax.fori_loop(0, NT // 2, prepare, 0)
+    def prepare_some(n):
+        lax.fori_loop(NT // 4 * n, NT // 4 * (n + 1), prepare, 0)
+
+    local[0].wait()
+    pl.semaphore_wait(barrier, len(partners))
+    g_hub_start(0, masked(xt, 0))
+    g_start(0, xt, 0)
+    local[1].wait()
+    both = xt[0 : 2 * K, :]
+    gram = nt(both, both)
+    a_start(0, jnp.concatenate([gram[:K], gram[K:]], axis=1))
+    table_v[...] = plan(band_rows, band_cols, hub_rows, hub_slots)
+    to_smem = pltpu.make_async_copy(table_v, table, lsem.at[5])
+    to_smem.start()
+    for n in (2, 3, 4):
+        local[n].wait()
+    prepare_some(0)
+    g_hub(0)
     a_z(0)
-    lax.fori_loop(NT // 2, NT, prepare, 0)
+    prepare_some(1)
+    g_panel(0)
+    g_hub_start(1, masked(xt, K))
+    g_start(1, xt, K)
+    prepare_some(2)
+    g_spread(0)
+    prepare_some(3)
+    a_x(0)
+    g_hub(1)
     to_smem.wait()
-    g_panel(0)
-    g_spread(0)
     g_halo(0)
-    g_band_end(0)
+    g_panel_end(0)
+    g_halo_end(0)
     multiply(0, band[0], 0, TPD)
+    g_panel(1)
+    a_back(0)
     g_pass(0)
-    g_start(1, xt, K)
     g_hub_end(0)
     multiply(0, hub[0], TPD, HTD)
-    a_x(0)
-    g_hub(1)
 
     def first_rows(r):
         return [row_sum(0, r + j) for j in range(OWN)]
 
-    scatter_start(0, first_rows)
-    a_back(0)
-    g_panel(1)
-    xt[2 * K :] = xt[0:K] - scatter_end(0, first_rows)
-    pay[1] = moments(xt)
-    a_start(1)
+    g_hub_start(2, row_sum(0, hub_row))
+    kept = scatter_start(0, first_rows)
+    g_spread(1)
+    g_panel_end(1)
+    a_start(1, panel_cross(lambda r: row_sum(0, r), (0, 1)))
+    g_hub(2, hub[0][d, pl.ds(HALF * c, HALF)])
+    g_halo(1)
+    sums = a_end(0)
+    gvd = jnp.concatenate([sums[:, : 2 * K], sums[:, 2 * K :]], axis=0)
+    w = xt[0:K] - scatter_end(0, kept)
+    xt[2 * K :] = w
+    w_start(0, w)
     g_start(2, xt, 2 * K)
-    sums0 = a_end(0)
-    gvd = jnp.concatenate([sums0[:, : 2 * K], sums0[:, 2 * K :]], axis=0)
-    g_spread(1)
-    g_halo(1)
+    w_plane(0)
     a_z(1)
-    g_hub(2)
-    g_band_end(1)
+    g_spread(2)
+    g_halo_end(1)
     multiply(1, band[1], 0, TPD)
+    g_pass(1)
+    w_z(0)
     a_x(1)
     g_panel(2)
-    g_pass(1)
-    a_back(1)
-    g_spread(2)
-    g_halo(2)
     g_hub_end(1)
     multiply(1, hub[1], TPD, HTD)
-    g_band_end(2)
-    multiply(2, band[2], 0, TPD)
-    sums1 = a_end(1)
-    mix, upper, lower = coefficients(0, gvd, sums1)
+    a_back(1)
+    w_back(0)
+    g_halo(2)
+    cross = gvd[:K] - a_end(1)
+    yall, zall, upper, left = prepared(0, gvd, cross)
     g_pass(2)
+    lower = jnp.concatenate([cross, w_end(0)], axis=1)
+    mix = coefficients(yall, zall, left, lower)
     mix_high, mix_low = split(mix[:K])
     mix_both = jnp.concatenate([mix_high, mix_low], axis=0)
-    xt2[0 : 2 * K] = nn(mix, xt[...])
-    carried = jnp.concatenate([nn(mix, upper), nt(mix, lower)], axis=1)
-    gvd = nt(carried, mix)
+    g_panel_end(2)
+    g_halo_end(2)
+    multiply(2, band[2], 0, TPD)
     g_hub_end(2)
     multiply(2, hub[2], TPD, HTD)
 
@@ -439,21 +515,29 @@
         one = jnp.dot(mix_both, high, preferred_element_type=F32)
         two = jnp.dot(mix_high, low, preferred_element_type=F32)
         out = one[:K] + one[K:] + two
-        return [out[:, TB * j : TB * (j + 1)] for j in range(OWN)]
-
-    scatter_start(1, second_rows)
-    xt2[2 * K :] = xt2[0:K] - scatter_end(1, second_rows)
-    pay[2] = moments(xt2)
-    a_start(2)
+        blocks = [out[:, TB * j : TB * (j + 1)] for j in range(OWN)]
+        for j in range(OWN):
+            mixed[r + j] = blocks[j]
+        return blocks
+
+    kept = scatter_start(1, second_rows)
+    a_start(2, nt(panel_cross(lambda r: mixed[r], (0, 1, 2)), mix[:, : K * 3]))
+    xt2[0 : 2 * K] = nn(mix, xt[...])
+    carried = jnp.concatenate([nn(mix, upper), nt(mix, lower)], axis=1)
+    gvd = nt(carried, mix)
+    w = xt2[0:K] - scatter_end(1, kept)
+    xt2[2 * K :] = w
+    w_start(1, w)
     a_z(2)
+    w_plane(1)
     a_x(2)
+    w_z(1)
     a_back(2)
-    sums2 = a_end(2)
-    ritz_out[...] = sums2[:, :K].T
-    mix2, _, _ = coefficients(1, gvd, sums2)
-    final = nn(mix2, xt2[...])
-    vec_out[...] = final[:K]
-    dir_out[...] = final[K:]
+    w_back(1)
+    cross = gvd[:K] - a_end(2)
+    ritz_out[...] = cross[:, :K]
+    yall, zall, upper, left = prepared(1, gvd, cross)
+    mix_out[...] = coefficients(yall, zall, left, jnp.concatenate([cross, w_end(1)], axis=1))
 
     for item in pending:
         if isinstance(item, tuple):
@@ -461,6 +545,13 @@
             pltpu.make_async_copy(ref, ref, ssem.at[sem]).wait()
         else:
             item.wait_send()
+
+
+def finish(mix, state, ritz, vec_out, dir_out, ritz_out):
+    whole = state[...]
+    vec_out[...] = nn(mix[:K], whole)
+    dir_out[...] = nn(mix[K:], whole)
+    ritz_out[...] = ritz[...].T
 
 
 def per_device(
@@ -472,11 +563,11 @@
     hbm = pl.BlockSpec(memory_space=pltpu.HBM)
     rows = start_vectors.shape[0]
     ext = [pltpu.VMEM((EXT, K, TB), F32)] * 3 + [pltpu.VMEM((HUBS, K, TB), F32)] * 3
-    vec, direc, ritz = pl.pallas_call(
+    mix, state, ritz = pl.pallas_call(
         kernel,
         out_shape=(
-            jax.ShapeDtypeStruct((K, rows), F32),
-            jax.ShapeDtypeStruct((K, rows), F32),
+            jax.ShapeDtypeStruct((2 * K, 3 * K), F32),
+            jax.ShapeDtypeStruct((3 * K, rows), F32),
             jax.ShapeDtypeStruct((K, K), F32),
         ),
         in_specs=[smem] * 5 + [hbm] * 5,
@@ -488,25 +579,27 @@
             pltpu.SMEM((NT, TB), jnp.int32),
             pltpu.VMEM((ITERS, K, 3 * K), F32),
             pltpu.VMEM((3 * K, rows), F32),
-            pltpu.VMEM((3 * K, rows), F32),
             pltpu.VMEM((3, OWN, K, TB), F32),
             pltpu.VMEM((3, K, TB), F32),
-            pltpu.VMEM((3, N_COL, 8, TB), F32),
-            pltpu.VMEM((3, N_DOM, 8, TB), F32),
+            pltpu.VMEM((3, N_COL, HALF, TB), F32),
+            pltpu.VMEM((3, NZ, HALF, TB), F32),
             *ext,
             *[pltpu.VMEM((NT, K, TB), F32)] * 3,
-            pltpu.VMEM((ITERS, NY, OWN, K, TB), F32),
-            pltpu.VMEM((ITERS, NY, OWN, K, TB), F32),
-            pltpu.VMEM((ITERS, NY, OWN, K, TB), F32),
-            pltpu.VMEM((ITERS, NY, OWN, K, TB), F32),
-            pltpu.VMEM((ITERS + 1, K, 4 * K), F32),
-            pltpu.VMEM((ITERS + 1, N_COL, 8, 4 * K), F32),
-            pltpu.VMEM((ITERS + 1, NZ, 8, 4 * K), F32),
-            pltpu.VMEM((ITERS + 1, NX, 8, 4 * K), F32),
-            pltpu.VMEM((ITERS + 1, N_COL, 8, 4 * K), F32),
+            pltpu.VMEM((PB, K, TB), F32),
+            *[pltpu.VMEM((ITERS, NY, OWN, K, TB), F32)] * 4,
+            *[
+                pltpu.VMEM((count,) + shape + (width,), F32)
+                for count, width in ((1, 4 * K), (ITERS, 2 * K))
+                for shape in ((K,), (N_COL, 8), (NZ, 8), (NX, 8), (N_COL, 8))
+            ],
+            pltpu.VMEM((ITERS, K // 2, 2 * K), F32),
+            pltpu.VMEM((ITERS, K // 4, 2 * K), F32),
+            pltpu.VMEM((ITERS, NX * NY, K // 4, 2 * K), F32),
+            pltpu.VMEM((ITERS, NZ, K // 4, 2 * K), F32),
+            pltpu.VMEM((ITERS, K // 2, 2 * K), F32),
             pltpu.SemaphoreType.DMA((6,)),
-            pltpu.SemaphoreType.DMA((100,)),
-            pltpu.SemaphoreType.DMA((100,)),
+            pltpu.SemaphoreType.DMA((120,)),
+            pltpu.SemaphoreType.DMA((120,)),
         ],
         compiler_params=pltpu.CompilerParams(
             collective_id=0, has_side_effects=True, vmem_limit_bytes=56 * 1024 * 1024
@@ -516,6 +609,17 @@
         band_rows, band_cols, hub_rows, hub_slots, hub_blocks, start_vectors.T, prior_directions.T,
         jnp.transpose(rotation, (0, 2, 1)), band_tiles, hub_tiles,
     )
+    vec, direc, ritz = pl.pallas_call(
+        finish,
+        out_shape=(
+            jax.ShapeDtypeStruct((K, rows), F32),
+            jax.ShapeDtypeStruct((K, rows), F32),
+            jax.ShapeDtypeStruct((K, K), F32),
+        ),
+        in_specs=[vmem] * 3,
+        out_specs=(vmem, vmem, vmem),
+        name="finish",
+    )(mix, state, ritz)
     return vec.T, direc.T, ritz
 
 

time: 108 us -> 98.4 us (0.911)
  Pallas kernels: 103 us -> 97.7 us
  local copies, waits for them, and re-layouts: 4.51 us -> 0 us
    pallas_call x1 -> x2, Pallas kernels: 103 us -> 97.7 us  [the longest x1 95.4 us: per_device(): pl.pallas_call(kernel, out_shape=(jax.ShapeDtypeStruct((2 * K, 3 * K), F3...]
    unnamed x3 -> x0, local copies, waits for them, and re-layouts: 4.51 us -> none
where the time goes in v3:
time: 98.4 us; the launch traced here: 98.3 us
  Pallas kernels  97.7 us (99%)
    pallas_call x1, Pallas kernels, per_device(): pl.pallas_call(kernel, out_shape=(jax.ShapeDtypeStruct((2 * K, 3 * K), F3...  95.4 us
    pallas_call x1, Pallas kernels, per_device(): pl.pallas_call(finish, out_shape=(jax.ShapeDtypeStruct((K, rows), F32), j...  2.27 us

profile of v3, /device:TPU:1, one launch (start us, length us, event | category | flops | bytes accessed | tf_op | source)
XLA Modules:
  0.0 98.3 jit_solution(16848197669220464598)
XLA Ops:
  0.6 95.4 %lobpcg.1 = (f32[128,192]{1,0:T(8,128)}, f32[192,512]{1,0:T(8,128)}, f32[64,64]{1,0:T(8,128)}) custom-call(s32[24]{0:T(128)} %band_rows.1, s32[24]{0:T(128)} %band_cols.1, s32[8]{0:T(128)} %hub_rows.1, s32[8]{0:T(128)} %hub_slots.1, s32[32]{0:T(128)} %hub_blocks.1, f32[64,512]{1,0:T(8,128)} %bitcast.5, f32[64,512]{1,0:T(8,128)} %bitcast.6, ...), custom_call_target="tpu_custom_call" | custom-call | tf_op jit(solution)/shard_map/lobpcg/pallas_call | solution.py:566
  96.0 2.3 %finish.1 = (f32[64,512]{1,0:T(8,128)}, f32[64,512]{1,0:T(8,128)}, f32[64,64]{1,0:T(8,128)}) custom-call(f32[128,192]{1,0:T(8,128)} %get-tuple-element.9.mix, f32[192,512]{1,0:T(8,128)} %get-tuple-element.10.state, f32[64,64]{1,0:T(8,128)} %get-tuple-element.11.ritz), custom_call_target="tpu_custom_call" | custom-call | tf_op jit(solution)/shard_map/finish/pallas_call | solution.py:612

commit v4 on v3

--- a/solution.py
+++ b/solution.py
@@ -124,8 +124,9 @@
 
 
 def kernel(
-    band_rows, band_cols, hub_rows, hub_slots, hub_blocks, vec_hbm, dir_hbm, rot_hbm, band_hbm, hub_hbm,
+    blocks_hbm, rows_hbm, cols_hbm, hrows_hbm, slots_hbm, vec_hbm, dir_hbm, rot_hbm, band_hbm, hub_hbm,
     mix_out, xt2, ritz_out,
+    hub_blocks, band_rows, band_cols, hub_rows, hub_slots,
     tiles, weights, table_v, table, rot, xt,
     own, cand, hca, hubz, eb0, eb1, eb2, eh0, eh1, eh2, pr0, pr1, pr2, mixed,
     ssend, srecv, rsum, rrecv, pay0, ra0, rb0, rx0, rc0, pay1, ra1, rb1, rx1, rc1,
@@ -145,13 +146,26 @@
     def at_xz(i, k):
         return (wrap(x + i, NX) * NZ + wrap(z + k, NZ), q)
 
-    others = [(i, k) for i in range(NX) for k in range(NZ) if (i, k) != (0, 0)]
-    partners = [(d, wrap(q + k, N_COL)) for k in range(1, N_COL)] + [at_xz(i, k) for i, k in others]
+    def at_xy(i, k):
+        return (wrap(x + i, NX) * NZ + z, 2 * wrap(y + k, NY) + c)
+
+    plane = ((2, 2), (2, 1), (2, 3), (1, 2), (3, 2), (2, 0), (0, 2), (1, 1), (1, 3), (3, 1), (3, 3), (1, 0), (3, 0), (0, 1), (0, 3))
+    partners = [at_xz(0, k) for k in (4, 3, 5, 2, 6, 1, 7)] + [at_xz(i, 0) for i in (2, 1, 3)]
+    partners += [(wrap(d + 1, N_DOM), q), (wrap(d - 1, N_DOM), q)] + [(d, wrap(q + k, N_COL)) for k in range(1, N_COL)]
+
+    barrier = pltpu.get_barrier_semaphore()
+    for partner in partners:
+        pl.semaphore_signal(barrier, inc=1, device_id=partner, device_id_type=MESH)
 
     local = []
     for n, (src, dst) in enumerate(
         (
+            (blocks_hbm, hub_blocks),
             (vec_hbm, xt.at[pl.ds(0, K)]),
+            (rows_hbm, band_rows),
+            (cols_hbm, band_cols),
+            (hrows_hbm, hub_rows),
+            (slots_hbm, hub_slots),
             (dir_hbm, xt.at[pl.ds(K, K)]),
             (band_hbm, tiles.at[pl.ds(0, TPD)]),
             (hub_hbm, tiles.at[pl.ds(TPD, HTD)]),
@@ -160,16 +174,21 @@
     ):
         local.append(pltpu.make_async_copy(src, dst, lsem.at[n]))
         local[n].start()
-    barrier = pltpu.get_barrier_semaphore()
-    for partner in partners:
-        pl.semaphore_signal(barrier, inc=1, device_id=partner, device_id_type=MESH)
-
     counter = [0]
     pending = []
 
     def sems(n=1):
         counter[0] += n
         return counter[0] - n
+
+    def drain():
+        for item in pending:
+            if isinstance(item, tuple):
+                ref, sem = item
+                pltpu.make_async_copy(ref, ref, ssem.at[sem]).wait()
+            else:
+                item.wait_send()
+        pending.clear()
 
     def send(src, dst, sem, device):
         copy = pltpu.make_async_remote_copy(
@@ -185,9 +204,10 @@
     def block_of(col):
         return pl.ds(HW + OWN * col, OWN)
 
+    local[0].wait()
     mask = [jnp.where(hub_blocks[d] - d * PB - q * OWN == j, 1.0, 0.0) for j in range(OWN)]
     names = ("ha", "p", "hb", "pf", "h", "hc", "hcf")
-    gsem = [dict(zip(names, [sems(n) for n in (1, NY, 1, NY, 4, NX, NX)])) for _ in range(3)]
+    gsem = [dict(zip(names, [sems(n) for n in (1, NY, NZ, NY, 4, NX, NX)])) for _ in range(3)]
     hub_row = jnp.clip(hub_blocks[d] - d * PB, 0, PB - 1)
 
     def g_start(g, ref, first):
@@ -221,8 +241,8 @@
             piece = piece + hca[g, k]
         hubz[g, z] = piece if base is None else base - piece
         for k in (4, 3, 5, 2, 6, 1, 7):
-            send(hubz.at[g, z], hubz.at[g, z], gsem[g]["hb"], at_xz(0, k))
-        pending.append((hubz.at[g, pl.ds(0, NZ - 1)], gsem[g]["hb"]))
+            pending.append(send(hubz.at[g, z], hubz.at[g, z], gsem[g]["hb"] + k, at_xz(0, k)))
+        hub_on(g, z)
 
     def g_panel(g):
         for k in (1, 3, 2):
@@ -236,14 +256,21 @@
     def slab(g, at_x, half):
         return hub[g].at[pl.ds(NZ * at_x, NZ), pl.ds(HALF * half, HALF)]
 
-    def g_spread(g):
-        arrived(hubz.at[g, pl.ds(0, NZ - 1)], gsem[g]["hb"])
-        mine = slab(g, x, c)
+    def hub_on(g, at_z):
+        mine = hub[g].at[NZ * x + at_z, pl.ds(HALF * c, HALF)]
         for i in (2, 1, 3):
-            pending.append(send(hubz.at[g], mine, gsem[g]["hc"] + i, at_xz(i, 0)))
-        pending.append(send(hubz.at[g], mine, gsem[g]["hcf"], sib))
-        for s in range(NZ):
-            hub[g][NZ * x + s, pl.ds(HALF * c, HALF)] = hubz[g, s]
+            send(hubz.at[g, at_z], mine, gsem[g]["hc"] + i, at_xz(i, 0))
+        hub[g][NZ * x + at_z, pl.ds(HALF * c, HALF)] = hubz[g, at_z]
+
+    def g_spread(g, part=None):
+        near = (1, 7, 2, 6), (3, 5, 4)
+        for k in near[0] + near[1] if part is None else near[part]:
+            at_z = wrap(z - k, NZ)
+            arrived(hubz.at[g, at_z], gsem[g]["hb"] + k)
+            hub_on(g, at_z)
+        if part != 0:
+            pending.extend((hubz.at[g], gsem[g]["hc"] + i) for i in (1, 2, 3))
+            pending.append(send(hubz.at[g], slab(g, x, c), gsem[g]["hcf"], sib))
 
     def g_halo(g):
         for n, at in enumerate((OWN * c, HW + PB + OWN * c)):
@@ -279,7 +306,8 @@
                     [jnp.concatenate([high, high], axis=1), jnp.concatenate([low, jnp.zeros_like(low)], axis=1)], axis=0
                 )
                 both = jnp.dot(left, weights[table[t, 0]], preferred_element_type=F32)
-                total = total * table[t, 2].astype(F32) + (both[:K] + both[K:])
+                product = both[:K] + both[K:]
+                total = total * table[t, 2].astype(F32) + product
                 prods[g][t] = total
             return total
 
@@ -311,16 +339,23 @@
             blocks = [block + rrecv[n, k, j] for j, block in enumerate(blocks)]
         return jnp.concatenate(blocks, axis=1)
 
+    def cross_of(blocks, groups, at):
+        highs, lows = zip(*[split(block) for block in blocks])
+        there = [split(jnp.concatenate([band[g][HW + r] for g in groups], axis=0)) for r in at]
+        left, right = [], []
+        for ph, pl_, (gh, gl) in zip(highs, lows, there):
+            left += [ph, ph, pl_]
+            right += [gh, gl, gh]
+        return lax.dot_general(
+            jnp.concatenate(left, axis=1), jnp.concatenate(right, axis=1), (((1,), (1,)), ((), ())),
+            preferred_element_type=F32,
+        )
+
     def panel_cross(block_at, groups):
         def some(n, total):
-            for u in range(4):
-                r = 4 * n + u
-                ph, pl_ = split(block_at(r))
-                gh, gl = split(jnp.concatenate([band[g][HW + r] for g in groups], axis=0))
-                total = total + lax.dot_general(
-                    jnp.concatenate([ph, ph, pl_], axis=1), jnp.concatenate([gh, gl, gh], axis=1),
-                    (((1,), (1,)), ((), ())), preferred_element_type=F32,
-                )
+            for u in range(0, 4, 2):
+                at = (4 * n + u, 4 * n + u + 1)
+                total = total + cross_of([block_at(r) for r in at], groups, at)
             return total
 
         return lax.fori_loop(0, PB // 4, some, jnp.zeros((K, K * len(groups)), F32))
@@ -384,9 +419,8 @@
         arrived(wrecv.at[n], wsems[n])
         at = x * NY + y
         wplane[n, at] = wpay[n, pl.ds(16 * c, 16)] + wrecv[n]
-        for i, k in ((2, 2), (2, 1), (2, 3), (1, 2), (3, 2), (2, 0), (0, 2), (1, 1), (1, 3), (3, 1), (3, 3), (1, 0), (3, 0), (0, 1), (0, 3)):
-            peer = (wrap(x + i, NX) * NZ + z, 2 * wrap(y + k, NY) + c)
-            send(wplane.at[n, at], wplane.at[n, at], wsems[n] + 1, peer)
+        for i, k in plane:
+            send(wplane.at[n, at], wplane.at[n, at], wsems[n] + 1, at_xy(i, k))
         pending.append((wplane.at[n, pl.ds(0, NX * NY - 1)], wsems[n] + 1))
 
     def w_z(n):
@@ -428,75 +462,78 @@
     def prepare_some(n):
         lax.fori_loop(NT // 4 * n, NT // 4 * (n + 1), prepare, 0)
 
-    local[0].wait()
+    local[1].wait()
     pl.semaphore_wait(barrier, len(partners))
     g_hub_start(0, masked(xt, 0))
     g_start(0, xt, 0)
-    local[1].wait()
+    local[6].wait()
     both = xt[0 : 2 * K, :]
     gram = nt(both, both)
     a_start(0, jnp.concatenate([gram[:K], gram[K:]], axis=1))
+    for n in (2, 3, 4, 5):
+        local[n].wait()
     table_v[...] = plan(band_rows, band_cols, hub_rows, hub_slots)
-    to_smem = pltpu.make_async_copy(table_v, table, lsem.at[5])
+    to_smem = pltpu.make_async_copy(table_v, table, lsem.at[10])
     to_smem.start()
-    for n in (2, 3, 4):
+    for n in (7, 8, 9):
         local[n].wait()
     prepare_some(0)
     g_hub(0)
+    prepare_some(1)
     a_z(0)
-    prepare_some(1)
     g_panel(0)
+    g_spread(0, 0)
     g_hub_start(1, masked(xt, K))
     g_start(1, xt, K)
     prepare_some(2)
-    g_spread(0)
-    prepare_some(3)
+    g_spread(0, 1)
     a_x(0)
-    g_hub(1)
     to_smem.wait()
     g_halo(0)
     g_panel_end(0)
     g_halo_end(0)
     multiply(0, band[0], 0, TPD)
+    prepare_some(3)
+    g_pass(0)
+    g_hub(1)
     g_panel(1)
     a_back(0)
-    g_pass(0)
     g_hub_end(0)
     multiply(0, hub[0], TPD, HTD)
 
     def first_rows(r):
         return [row_sum(0, r + j) for j in range(OWN)]
 
+    kept = scatter_start(0, first_rows)
     g_hub_start(2, row_sum(0, hub_row))
-    kept = scatter_start(0, first_rows)
-    g_spread(1)
     g_panel_end(1)
     a_start(1, panel_cross(lambda r: row_sum(0, r), (0, 1)))
     g_hub(2, hub[0][d, pl.ds(HALF * c, HALF)])
+    g_spread(1)
     g_halo(1)
     sums = a_end(0)
     gvd = jnp.concatenate([sums[:, : 2 * K], sums[:, 2 * K :]], axis=0)
+    a_z(1)
     w = xt[0:K] - scatter_end(0, kept)
     xt[2 * K :] = w
     w_start(0, w)
     g_start(2, xt, 2 * K)
     w_plane(0)
-    a_z(1)
-    g_spread(2)
     g_halo_end(1)
     multiply(1, band[1], 0, TPD)
+    a_x(1)
+    g_spread(2)
     g_pass(1)
-    w_z(0)
-    a_x(1)
-    g_panel(2)
     g_hub_end(1)
     multiply(1, hub[1], TPD, HTD)
     a_back(1)
-    w_back(0)
-    g_halo(2)
+    w_z(0)
+    g_panel(2)
     cross = gvd[:K] - a_end(1)
     yall, zall, upper, left = prepared(0, gvd, cross)
+    w_back(0)
     g_pass(2)
+    g_halo(2)
     lower = jnp.concatenate([cross, w_end(0)], axis=1)
     mix = coefficients(yall, zall, left, lower)
     mix_high, mix_low = split(mix[:K])
@@ -525,10 +562,11 @@
     xt2[0 : 2 * K] = nn(mix, xt[...])
     carried = jnp.concatenate([nn(mix, upper), nt(mix, lower)], axis=1)
     gvd = nt(carried, mix)
+    drain()
+    a_z(2)
     w = xt2[0:K] - scatter_end(1, kept)
     xt2[2 * K :] = w
     w_start(1, w)
-    a_z(2)
     w_plane(1)
     a_x(2)
     w_z(1)
@@ -537,14 +575,10 @@
     cross = gvd[:K] - a_end(2)
     ritz_out[...] = cross[:, :K]
     yall, zall, upper, left = prepared(1, gvd, cross)
+    drain()
     mix_out[...] = coefficients(yall, zall, left, jnp.concatenate([cross, w_end(1)], axis=1))
 
-    for item in pending:
-        if isinstance(item, tuple):
-            ref, sem = item
-            pltpu.make_async_copy(ref, ref, ssem.at[sem]).wait()
-        else:
-            item.wait_send()
+    drain()
 
 
 def finish(mix, state, ritz, vec_out, dir_out, ritz_out):
@@ -558,7 +592,6 @@
     band_tiles, band_rows, band_cols, hub_tiles, hub_rows, hub_slots, hub_blocks,
     start_vectors, prior_directions, rotation,
 ):
-    smem = pl.BlockSpec(memory_space=pltpu.SMEM)
     vmem = pl.BlockSpec(memory_space=pltpu.VMEM)
     hbm = pl.BlockSpec(memory_space=pltpu.HBM)
     rows = start_vectors.shape[0]
@@ -570,9 +603,10 @@
             jax.ShapeDtypeStruct((3 * K, rows), F32),
             jax.ShapeDtypeStruct((K, K), F32),
         ),
-        in_specs=[smem] * 5 + [hbm] * 5,
+        in_specs=[hbm] * 10,
         out_specs=(vmem, vmem, vmem),
         scratch_shapes=[
+            *[pltpu.SMEM((count,), jnp.int32) for count in (HUBS, TPD, TPD, HTD, HTD)],
             pltpu.VMEM((NT, TB, TB), F32),
             pltpu.VMEM((NT, 2 * TB, TB), BF16),
             pltpu.VMEM((NT, TB), jnp.int32),
@@ -597,16 +631,16 @@
             pltpu.VMEM((ITERS, NX * NY, K // 4, 2 * K), F32),
             pltpu.VMEM((ITERS, NZ, K // 4, 2 * K), F32),
             pltpu.VMEM((ITERS, K // 2, 2 * K), F32),
-            pltpu.SemaphoreType.DMA((6,)),
-            pltpu.SemaphoreType.DMA((120,)),
-            pltpu.SemaphoreType.DMA((120,)),
+            pltpu.SemaphoreType.DMA((11,)),
+            pltpu.SemaphoreType.DMA((128,)),
+            pltpu.SemaphoreType.DMA((128,)),
         ],
         compiler_params=pltpu.CompilerParams(
             collective_id=0, has_side_effects=True, vmem_limit_bytes=56 * 1024 * 1024
         ),
         name="lobpcg",
     )(
-        band_rows, band_cols, hub_rows, hub_slots, hub_blocks, start_vectors.T, prior_directions.T,
+        hub_blocks, band_rows, band_cols, hub_rows, hub_slots, start_vectors.T, prior_directions.T,
         jnp.transpose(rotation, (0, 2, 1)), band_tiles, hub_tiles,
     )
     vec, direc, ritz = pl.pallas_call(

time: 98.4 us -> 96.1 us (0.977)
  Pallas kernels: 97.7 us -> 95.4 us
    pallas_call x1, Pallas kernels: 95.4 us -> 93.1 us  [per_device(): pl.pallas_call(kernel, out_shape=(jax.ShapeDtypeStruct((2 * K, 3 * K), F3...]
where the time goes in v4:
time: 96.1 us; the launch traced here: 96 us
  Pallas kernels  95.4 us (99%)
    pallas_call x1, Pallas kernels, per_device(): pl.pallas_call(kernel, out_shape=(jax.ShapeDtypeStruct((2 * K, 3 * K), F3...  93.1 us
    pallas_call x1, Pallas kernels, per_device(): pl.pallas_call(finish, out_shape=(jax.ShapeDtypeStruct((K, rows), F32), j...  2.27 us

profile of v4, /device:TPU:1, one launch (start us, length us, event | category | flops | bytes accessed | tf_op | source)
XLA Modules:
  0.0 96.0 jit_solution(11563614079223562280)
XLA Ops:
  0.6 93.1 %lobpcg.1 = (f32[128,192]{1,0:T(8,128)}, f32[192,512]{1,0:T(8,128)}, f32[64,64]{1,0:T(8,128)}) custom-call(s32[32]{0:T(128)} %blocks_hbm.1, s32[24]{0:T(128)} %rows_hbm.1, s32[24]{0:T(128)} %cols_hbm.1, s32[8]{0:T(128)} %hrows_hbm.1, s32[8]{0:T(128)} %slots_hbm.1, f32[64,512]{1,0:T(8,128)} %bitcast.5, f32[64,512]{1,0:T(8,128)} %bitcast.6, ...), custom_call_target="tpu_custom_call" | custom-call | tf_op jit(solution)/shard_map/lobpcg/pallas_call | solution.py:599
  93.8 2.3 %finish.1 = (f32[64,512]{1,0:T(8,128)}, f32[64,512]{1,0:T(8,128)}, f32[64,64]{1,0:T(8,128)}) custom-call(f32[128,192]{1,0:T(8,128)} %get-tuple-element.9.mix, f32[192,512]{1,0:T(8,128)} %get-tuple-element.10.state, f32[64,64]{1,0:T(8,128)} %get-tuple-element.11.ritz), custom_call_target="tpu_custom_call" | custom-call | tf_op jit(solution)/shard_map/finish/pallas_call | solution.py:646

commit v5 on v4

--- a/solution.py
+++ b/solution.py
@@ -318,11 +318,13 @@
 
     ssems = [(sems(NY), sems(NY)) for _ in range(ITERS)]
 
-    def scatter_start(n, rows_of):
+    def scatter_start(n, rows_of, between=None):
         for k in (2, 1, 3, 0):
             for j, block in enumerate(rows_of(OWN * (2 * wrap(y + k, NY) + other))):
                 ssend[n, k, j] = block
             pending.append(send(ssend.at[n, k], srecv.at[n, k], ssems[n][0] + k, sib))
+        if between is not None:
+            between()
         for k in (2, 1, 3):
             blocks = rows_of(OWN * (2 * wrap(y + k, NY) + c))
             arrived(srecv.at[n, k], ssems[n][0] + k)
@@ -504,25 +506,26 @@
     def first_rows(r):
         return [row_sum(0, r + j) for j in range(OWN)]
 
-    kept = scatter_start(0, first_rows)
-    g_hub_start(2, row_sum(0, hub_row))
+    kept = scatter_start(0, first_rows, lambda: g_hub_start(2, row_sum(0, hub_row)))
     g_panel_end(1)
-    a_start(1, panel_cross(lambda r: row_sum(0, r), (0, 1)))
+    crossed = panel_cross(lambda r: row_sum(0, r), (0, 1))
     g_hub(2, hub[0][d, pl.ds(HALF * c, HALF)])
+    a_start(1, crossed)
     g_spread(1)
     g_halo(1)
     sums = a_end(0)
     gvd = jnp.concatenate([sums[:, : 2 * K], sums[:, 2 * K :]], axis=0)
     a_z(1)
+    g_spread(2, 0)
     w = xt[0:K] - scatter_end(0, kept)
     xt[2 * K :] = w
     w_start(0, w)
     g_start(2, xt, 2 * K)
     w_plane(0)
+    g_spread(2, 1)
     g_halo_end(1)
     multiply(1, band[1], 0, TPD)
     a_x(1)
-    g_spread(2)
     g_pass(1)
     g_hub_end(1)
     multiply(1, hub[1], TPD, HTD)

time: 96.1 us -> 95 us (0.989)
  Pallas kernels: 95.4 us -> 94.2 us
    pallas_call x1, Pallas kernels: 93.1 us -> 92 us  [per_device(): pl.pallas_call(kernel, out_shape=(jax.ShapeDtypeStruct((2 * K, 3 * K), F3...]
where the time goes in v5:
time: 95 us; the launch traced here: 94.9 us
  Pallas kernels  94.2 us (99%)
    pallas_call x1, Pallas kernels, per_device(): pl.pallas_call(kernel, out_shape=(jax.ShapeDtypeStruct((2 * K, 3 * K), F3...  92 us
    pallas_call x1, Pallas kernels, per_device(): pl.pallas_call(finish, out_shape=(jax.ShapeDtypeStruct((K, rows), F32), j...  2.27 us

profile of v5, /device:TPU:1, one launch (start us, length us, event | category | flops | bytes accessed | tf_op | source)
XLA Modules:
  0.0 94.9 jit_solution(15196201347722091726)
XLA Ops:
  0.6 92.0 %lobpcg.1 = (f32[128,192]{1,0:T(8,128)}, f32[192,512]{1,0:T(8,128)}, f32[64,64]{1,0:T(8,128)}) custom-call(s32[32]{0:T(128)} %blocks_hbm.1, s32[24]{0:T(128)} %rows_hbm.1, s32[24]{0:T(128)} %cols_hbm.1, s32[8]{0:T(128)} %hrows_hbm.1, s32[8]{0:T(128)} %slots_hbm.1, f32[64,512]{1,0:T(8,128)} %bitcast.5, f32[64,512]{1,0:T(8,128)} %bitcast.6, ...), custom_call_target="tpu_custom_call" | custom-call | tf_op jit(solution)/shard_map/lobpcg/pallas_call | solution.py:602
  92.6 2.3 %finish.1 = (f32[64,512]{1,0:T(8,128)}, f32[64,512]{1,0:T(8,128)}, f32[64,64]{1,0:T(8,128)}) custom-call(f32[128,192]{1,0:T(8,128)} %get-tuple-element.9.mix, f32[192,512]{1,0:T(8,128)} %get-tuple-element.10.state, f32[64,64]{1,0:T(8,128)} %get-tuple-element.11.ritz), custom_call_target="tpu_custom_call" | custom-call | tf_op jit(solution)/shard_map/finish/pallas_call | solution.py:649
